TPU v7x, 512 devices: a whole 4x4x16 slice. The times are simulated.
512 devices in a mesh: ctx: 64 (over y, x, z_hi), img: 8 (over z_lo, core).
Axes of the slice: x: 4, y: 4, z: 16 (z_hi: 4, z_lo: 4; z = z_hi * 4 + z_lo), core: 2. Of those that a mesh axis runs over, the one named last changes fastest.
Arguments:
- self_query_rows: bfloat16 [8192, 8192], P('ctx', 'img'), may hold values from -128 to 128
- text_key_value: bfloat16 [8192, 2, 1024], P('ctx', None, 'img'), may hold values from -16 to 16
- cross_query_rows: bfloat16 [8192, 8192], P('ctx', 'img'), may hold values from -128 to 128
- vision_key_value: bfloat16 [64, 64, 2, 1024], P('ctx', 'img'), may hold values from -16 to 16
- doc_start: int32 [128], P('ctx'), may hold values from 0 to 8128, as said below
- image_mask: int32 [128, 64], P('ctx'), may hold values from 0 to 1, as said below
Outputs:
- self_out: bfloat16 [8192, 8192], P('ctx', 'img')
- cross_out: bfloat16 [8192, 8192], P('ctx', 'img')
Inputs may be any that keep to these rules, and one draw needn't show every extreme that they name: Documents are runs of whole mask blocks: doc_start[b] is a multiple of 64, at most b * 64, never falls from one block to the next, and is 0 for the first block. `image_mask`: 1 where the text of mask block b may attend image i; every block may attend at least one image.
All inputs are finite; a program needn't handle non-finite values.
Results may differ from a plain program's by a relative error of at most 0.0049.
Values may be sent and summed in bfloat16 or wider, within the bound.
No kernel may reach another device: no remote copies, remote signals or barrier semaphores. Data moves between devices by JAX's collectives and lax.ppermute only.
A program may use at most 64 MiB of HBM per device.

v0:
```python
import math

import jax
import jax.numpy as jnp
from jax import lax
from jax.sharding import PartitionSpec as P

QUERY_HEADS = 64
KEY_VALUE_HEADS = 8
HEAD_WIDTH = 128
MBLK = 64


NEGATIVE = -1e30


def attend(carry, queries, key_block, value_block, allowed, factor):
    top_score, totals, output = carry
    scores = (
        jnp.einsum("tkgd,skd->tkgs", queries, key_block, preferred_element_type=jnp.float32)
        * factor
    )
    visible = allowed[:, None, None, :]
    scores = jnp.where(visible, scores, NEGATIVE)
    new_top = jnp.maximum(top_score, jnp.max(scores, axis=-1))
    weights = jnp.where(visible, jnp.exp(scores - new_top[..., None]), 0.0)
    shrink = jnp.exp(top_score - new_top)
    totals = totals * shrink + jnp.sum(weights, axis=-1)
    output = output * shrink[..., None] + jnp.einsum(
        "tkgs,skd->tkgd",
        weights.astype(jnp.bfloat16),
        value_block,
        preferred_element_type=jnp.float32,
    )
    return (new_top, totals, output)


def update(carry, queries, key_block, value_block, allowed, factor):
    return attend(carry, queries, key_block, value_block, allowed, factor)


def sweep(carry, queries, key_block, value_block, allowed, unit, factor):
    key_count = key_block.shape[0]
    pieces = key_count // unit
    per_block = math.gcd(pieces, max(1, 2048 // unit))
    block_rows = per_block * unit
    blocks = key_count // block_rows
    key_blocks = key_block.reshape(blocks, block_rows, key_block.shape[1], key_block.shape[2])
    value_blocks = value_block.reshape(
        blocks, block_rows, value_block.shape[1], value_block.shape[2]
    )
    mask_blocks = allowed.reshape(allowed.shape[0], blocks, block_rows).transpose(1, 0, 2)

    def one_step(running, inputs):
        return (update(running, queries, inputs[0], inputs[1], inputs[2], factor), None)

    carry, unused = lax.scan(one_step, carry, (key_blocks, value_blocks, mask_blocks))
    return carry


def body(
    self_query_rows, text_key_value, cross_query_rows, vision_key_value, doc_start, image_mask
):
    row_count = self_query_rows.shape[0]
    local_heads = text_key_value.shape[2] // HEAD_WIDTH
    group_width = QUERY_HEADS // KEY_VALUE_HEADS
    factor = HEAD_WIDTH ** (-0.5)
    first_row = lax.axis_index("ctx") * row_count
    self_queries = self_query_rows.reshape(row_count, local_heads, group_width, HEAD_WIDTH)
    cross_queries = cross_query_rows.reshape(row_count, local_heads, group_width, HEAD_WIDTH)
    positions = first_row + jnp.arange(row_count, dtype=jnp.int32)
    token_start = jnp.repeat(doc_start, MBLK)
    token_mask = jnp.repeat(image_mask, MBLK, axis=0) > 0
    per_device = vision_key_value.shape[0]
    head_rows = lax.all_to_all(vision_key_value, "img", split_axis=3, concat_axis=1, tiled=True)
    vision_piece = head_rows[None]
    text_piece = text_key_value[None]
    start_carry = (
        jnp.full((row_count, local_heads, group_width), NEGATIVE, jnp.float32),
        jnp.zeros((row_count, local_heads, group_width), jnp.float32),
        jnp.zeros((row_count, local_heads, group_width, HEAD_WIDTH), jnp.float32),
    )
    piece = lax.all_gather(vision_piece, "ctx", axis=0, tiled=True)
    shards = piece.shape[0]
    image_rows = piece.shape[2]
    key_count = shards * per_device * image_rows
    key_block = piece[:, :, :, 0].reshape(key_count, local_heads, HEAD_WIDTH)
    value_block = piece[:, :, :, 1].reshape(key_count, local_heads, HEAD_WIDTH)
    allowed = jnp.repeat(token_mask, image_rows, axis=1)
    cross_state = sweep(
        start_carry, cross_queries, key_block, value_block, allowed, per_device * image_rows, factor
    )
    piece = lax.all_gather(text_piece, "ctx", axis=0, tiled=True)
    shards = piece.shape[0]
    key_count = shards * row_count
    key_block = piece[:, :, 0].reshape(key_count, local_heads, HEAD_WIDTH)
    value_block = piece[:, :, 1].reshape(key_count, local_heads, HEAD_WIDTH)
    key_pos = jnp.arange(key_count, dtype=jnp.int32)
    allowed = (key_pos[None, :] <= positions[:, None]) & (key_pos[None, :] >= token_start[:, None])
    self_state = sweep(
        start_carry, self_queries, key_block, value_block, allowed, row_count, factor
    )

    def finish(running):
        return (
            (running[2] / running[1][..., None])
            .reshape(row_count, local_heads * group_width * HEAD_WIDTH)
            .astype(jnp.bfloat16)
        )

    return (finish(self_state), finish(cross_state))


def solution(mesh):
    placed = (
        P("ctx", "img"),
        P("ctx", None, "img"),
        P("ctx", "img"),
        P("ctx", "img", None, None),
        P("ctx"),
        P("ctx", None),
    )
    return jax.shard_map(
        body,
        mesh=mesh,
        in_specs=placed,
        out_specs=(P("ctx", "img"), P("ctx", "img")),
        check_vma=False,
    )
```

profile of v0, /device:TPU:1, one launch (start us, length us, event | category | flops | bytes accessed | tf_op | source)
XLA Modules:
  0.0 351.2 jit_solution(3317081169899329068)
XLA Ops:
  7.2 1.2 copy.55
  9.0 14.2 %all_to_all.15 = bf16[8,2,1024]{2,1,0:T(2,128)(2,1)S(1)} all-to-all(bf16[8,2,1024]{2,1,0:T(2,128)(2,1)S(1)} %reshape.127), channel_id=1, replica_groups=mesh['ctx'=64,'img'=8] {'img'}, dimensions={0} | all-to-all | bytes 65536 | tf_op jit(solution)/shard_map/all_to_all | solution.py:75
  29.8 3.1 compare_and_fusion
  33.0 107.8 %all-gather.4.cloned.1.call-done = bf16[64,1,64,2,128]{4,2,0,3,1:T(8,128)(2,1)} async-done(((bf16[1,1,64,2,128]{4,2,0,3,1:T(8,128)(2,1)}), bf16[64,1,64,2,128]{4,2,0,3,1:T(8,128)(2,1)}) %all-gather.4.cloned.1.call-update) | async-done | bytes 2097168 | tf_op jit(solution)/shard_map/all_gather | solution.py:83
  140.8 1.7 fusion.51
  142.6 27.8 %while.31 = (s32[]{:T(128)}, f32[128,1,8]{0,2,1:T(8,128)S(1)}, f32[128,1,8]{0,2,1:T(8,128)S(1)}, f32[128,1,8,128]{0,3,2,1:T(8,128)}, pred[2,128,2048]{1,2,0:T(8,...) while((s32[]{:T(128)}, f32[128,1,8]{0,2,1:T(8,128)S(1)}, ...), condition=%wide.region_7.8_spmd.clone, body=%wide.region_4.7_spmd.clone.sunk | while | flops 1101404160 | bytes 62455968 | solution.py:57
  142.7 4.6 %fusion.72 = (f32[128,8]{0,1:T(8,128)S(1)}, f32[2048,128,8]{1,0,2:T(8,128)}) fusion(pred[128,2048]{0,1:T(8,128)(4,1)S(1)} %dynamic-slice_bitcast_fusion.5, bf16[128,1,8,128]{3,0,2,1:T(8,128)(2,1)S(1)} %get-tuple-element.408, bf16[2,2048,1,128]{3,1,2,0:T(8,128)(2,1)S(1)} %get-tuple-element.407, s32[]{:T(128)S(6)} %copy.84), kind=kOutput, calls=%fused_computation.30.clone.1 | convolution fusion | flops 543161344 | bytes 9441284 | tf_op jit(solution)/shard_map/while/body/eval_jaxpr/tkgd,skd->tkgs/dot_general | solution.py:20
  147.3 4.6 %fusion.74 = f32[128,8]{0,1:T(8,128)S(1)} fusion(f32[2048,128,8]{1,0,2:T(8,128)} %get-tuple-element.350, f32[128,8]{0,1:T(8,128)S(1)} %bitcast.200, pred[128,2048]{0,1:T(8,128)(4,1)S(1)} %dynamic-slice_bitcast_fusion.5), kind=kLoop, calls=%fused_computation.32.clone.1 | loop fusion | flops 10484736 | bytes 8658944 | tf_op jit(solution)/shard_map/while/body/eval_jaxpr/reduce_sum | solution.py:28
  151.9 1.2 copy-done
  153.1 2.9 fusion.75
  156.0 4.6 %fusion.72 = (f32[128,8]{0,1:T(8,128)S(1)}, f32[2048,128,8]{1,0,2:T(8,128)}) fusion(pred[128,2048]{0,1:T(8,128)(4,1)S(1)} %dynamic-slice_bitcast_fusion.5, bf16[128,1,8,128]{3,0,2,1:T(8,128)(2,1)S(1)} %get-tuple-element.408, bf16[2,2048,1,128]{3,1,2,0:T(8,128)(2,1)S(1)} %get-tuple-element.407, s32[]{:T(128)S(6)} %copy.84), kind=kOutput, calls=%fused_computation.30.clone.1 | convolution fusion | flops 543161344 | bytes 9441284 | tf_op jit(solution)/shard_map/while/body/eval_jaxpr/tkgd,skd->tkgs/dot_general | solution.py:20
  160.7 4.6 %fusion.74 = f32[128,8]{0,1:T(8,128)S(1)} fusion(f32[2048,128,8]{1,0,2:T(8,128)} %get-tuple-element.350, f32[128,8]{0,1:T(8,128)S(1)} %bitcast.200, pred[128,2048]{0,1:T(8,128)(4,1)S(1)} %dynamic-slice_bitcast_fusion.5), kind=kLoop, calls=%fused_computation.32.clone.1 | loop fusion | flops 10484736 | bytes 8658944 | tf_op jit(solution)/shard_map/while/body/eval_jaxpr/reduce_sum | solution.py:28
  165.3 1.2 copy-done
  166.5 3.9 %fusion.75 = f32[128,1,8,128]{0,3,2,1:T(8,128)} fusion(f32[2048,128,8]{1,0,2:T(8,128)S(1)} %copy-done, f32[128,8]{0,1:T(8,128)S(1)} %bitcast.201, pred[128,2048]{0,1:T(8,128)(4,1)S(1)} %dynamic-slice_bitcast_fusion.5, f32[128,1,8,128]{0,3,2,1:T(8,128)} %get-tuple-element.395, bf16[2,2048,1,128]{3,1,0,2:T(8,128)(2,1)S(1)} %get-tuple-element.409, ...), kind=kOutput, calls=%fused_computation.37.clone.1 | convolution fusion | flops 547749888 | bytes 10231813 | tf_op jit(solution)/shard_map/while/body/eval_jaxpr/tkgs,skd->tkgd/dot_general | solution.py:29
  172.4 108.0 %all-gather.6.cloned.1.call-done = bf16[8192,2,128]{2,1,0:T(2,128)(2,1)} async-done(((bf16[128,2,128]{2,1,0:T(2,128)(2,1)}), bf16[8192,2,128]{2,1,0:T(2,128)(2,1)}) %all-gather.6.cloned.1.call-update) | async-done | bytes 4194320 | tf_op jit(solution)/shard_map/all_gather | solution.py:93
  280.4 2.7 copy.48
  283.1 1.7 fusion.50
  284.8 58.7 %while.30 = (s32[]{:T(128)}, f32[128,1,8]{0,2,1:T(8,128)S(1)}, f32[128,1,8]{0,2,1:T(8,128)S(1)}, f32[128,1,8,128]{0,3,2,1:T(8,128)S(1)}, pred[4,128,2048]{1,2,0:...) while((s32[]{:T(128)}, f32[128,1,8]{0,2,1:T(8,128)S(1)}, ...), condition=%wide.region_3.4_spmd.clone, body=%wide.region_0.3_spmd.clone.sunk | while | flops 1101404160 | bytes 62455968 | solution.py:57
  285.8 4.6 %fusion.66 = (f32[128,8]{0,1:T(8,128)S(1)}, f32[2048,128,8]{1,0,2:T(8,128)}) fusion(pred[128,2048]{0,1:T(8,128)(4,1)S(1)} %dynamic-slice_bitcast_fusion.4, bf16[128,1,8,128]{3,0,2,1:T(8,128)(2,1)S(1)} %get-tuple-element.378, bf16[4,2048,1,128]{3,1,2,0:T(8,128)(2,1)S(1)} %get-tuple-element.377, s32[]{:T(128)S(6)} %copy.72), kind=kOutput, calls=%fused_computation.2.clone.1 | convolution fusion | flops 543161344 | bytes 9441284 | tf_op jit(solution)/shard_map/while/body/eval_jaxpr/tkgd,skd->tkgs/dot_general | solution.py:20
  290.4 4.6 %fusion.68 = f32[128,8]{0,1:T(8,128)S(1)} fusion(f32[2048,128,8]{1,0,2:T(8,128)} %get-tuple-element.338, f32[128,8]{0,1:T(8,128)S(1)} %bitcast.202, pred[128,2048]{0,1:T(8,128)(4,1)S(1)} %dynamic-slice_bitcast_fusion.4), kind=kLoop, calls=%fused_computation.4.clone.1 | loop fusion | flops 10484736 | bytes 8658944 | tf_op jit(solution)/shard_map/while/body/eval_jaxpr/reduce_sum | solution.py:28
  295.1 1.2 copy-done.1
  296.2 3.2 fusion.69
  300.5 4.6 %fusion.66 = (f32[128,8]{0,1:T(8,128)S(1)}, f32[2048,128,8]{1,0,2:T(8,128)}) fusion(pred[128,2048]{0,1:T(8,128)(4,1)S(1)} %dynamic-slice_bitcast_fusion.4, bf16[128,1,8,128]{3,0,2,1:T(8,128)(2,1)S(1)} %get-tuple-element.378, bf16[4,2048,1,128]{3,1,2,0:T(8,128)(2,1)S(1)} %get-tuple-element.377, s32[]{:T(128)S(6)} %copy.72), kind=kOutput, calls=%fused_computation.2.clone.1 | convolution fusion | flops 543161344 | bytes 9441284 | tf_op jit(solution)/shard_map/while/body/eval_jaxpr/tkgd,skd->tkgs/dot_general | solution.py:20
  305.1 4.6 %fusion.68 = f32[128,8]{0,1:T(8,128)S(1)} fusion(f32[2048,128,8]{1,0,2:T(8,128)} %get-tuple-element.338, f32[128,8]{0,1:T(8,128)S(1)} %bitcast.202, pred[128,2048]{0,1:T(8,128)(4,1)S(1)} %dynamic-slice_bitcast_fusion.4), kind=kLoop, calls=%fused_computation.4.clone.1 | loop fusion | flops 10484736 | bytes 8658944 | tf_op jit(solution)/shard_map/while/body/eval_jaxpr/reduce_sum | solution.py:28
  309.7 1.2 copy-done.1
  310.9 3.2 fusion.69
  315.1 4.6 %fusion.66 = (f32[128,8]{0,1:T(8,128)S(1)}, f32[2048,128,8]{1,0,2:T(8,128)}) fusion(pred[128,2048]{0,1:T(8,128)(4,1)S(1)} %dynamic-slice_bitcast_fusion.4, bf16[128,1,8,128]{3,0,2,1:T(8,128)(2,1)S(1)} %get-tuple-element.378, bf16[4,2048,1,128]{3,1,2,0:T(8,128)(2,1)S(1)} %get-tuple-element.377, s32[]{:T(128)S(6)} %copy.72), kind=kOutput, calls=%fused_computation.2.clone.1 | convolution fusion | flops 543161344 | bytes 9441284 | tf_op jit(solution)/shard_map/while/body/eval_jaxpr/tkgd,skd->tkgs/dot_general | solution.py:20
  319.8 4.6 %fusion.68 = f32[128,8]{0,1:T(8,128)S(1)} fusion(f32[2048,128,8]{1,0,2:T(8,128)} %get-tuple-element.338, f32[128,8]{0,1:T(8,128)S(1)} %bitcast.202, pred[128,2048]{0,1:T(8,128)(4,1)S(1)} %dynamic-slice_bitcast_fusion.4), kind=kLoop, calls=%fused_computation.4.clone.1 | loop fusion | flops 10484736 | bytes 8658944 | tf_op jit(solution)/shard_map/while/body/eval_jaxpr/reduce_sum | solution.py:28
  325.6 3.2 fusion.69
  329.8 4.6 %fusion.66 = (f32[128,8]{0,1:T(8,128)S(1)}, f32[2048,128,8]{1,0,2:T(8,128)}) fusion(pred[128,2048]{0,1:T(8,128)(4,1)S(1)} %dynamic-slice_bitcast_fusion.4, bf16[128,1,8,128]{3,0,2,1:T(8,128)(2,1)S(1)} %get-tuple-element.378, bf16[4,2048,1,128]{3,1,2,0:T(8,128)(2,1)S(1)} %get-tuple-element.377, s32[]{:T(128)S(6)} %copy.72), kind=kOutput, calls=%fused_computation.2.clone.1 | convolution fusion | flops 543161344 | bytes 9441284 | tf_op jit(solution)/shard_map/while/body/eval_jaxpr/tkgd,skd->tkgs/dot_general | solution.py:20
  334.4 4.6 %fusion.68 = f32[128,8]{0,1:T(8,128)S(1)} fusion(f32[2048,128,8]{1,0,2:T(8,128)} %get-tuple-element.338, f32[128,8]{0,1:T(8,128)S(1)} %bitcast.202, pred[128,2048]{0,1:T(8,128)(4,1)S(1)} %dynamic-slice_bitcast_fusion.4), kind=kLoop, calls=%fused_computation.4.clone.1 | loop fusion | flops 10484736 | bytes 8658944 | tf_op jit(solution)/shard_map/while/body/eval_jaxpr/reduce_sum | solution.py:28
  340.3 3.2 fusion.69
  (63 shorter events, 16.5 us)
Async XLA Ops:
  7.2 133.6 %all-gather.4.cloned.1.call-start = ((), (), s32[]{:S(2)}) async-start(), calls=%async_computation.1 | async-start | bytes 2129920 | tf_op jit(solution)/shard_map/all_gather | solution.py:83
  24.8 255.7 %all-gather.6.cloned.1.call-start = ((), (), s32[]{:S(2)}) async-start(), calls=%async_computation.2 | async-start | bytes 4259840 | tf_op jit(solution)/shard_map/all_gather | solution.py:93
  147.3 5.8 %copy-start = (f32[2048,128,8]{1,0,2:T(8,128)S(1)}, f32[2048,128,8]{1,0,2:T(8,128)}, u32[]{:S(2)}) copy-start(f32[2048,128,8]{1,0,2:T(8,128)} %get-tuple-element.350) | copy-start | bytes 25165828 | tf_op jit(solution)/shard_map/while
  160.6 5.8 %copy-start = (f32[2048,128,8]{1,0,2:T(8,128)S(1)}, f32[2048,128,8]{1,0,2:T(8,128)}, u32[]{:S(2)}) copy-start(f32[2048,128,8]{1,0,2:T(8,128)} %get-tuple-element.350) | copy-start | bytes 25165828 | tf_op jit(solution)/shard_map/while
  172.4 112.4 %copy-start.2 = (f32[128,1,8,128]{0,3,2,1:T(8,128)S(1)}, f32[128,1,8,128]{0,3,2,1:T(8,128)}, u32[]{:S(2)}) copy-start(f32[128,1,8,128]{0,3,2,1:T(8,128)} %custom-call.2) | copy-start | bytes 1572868
  290.4 5.8 %copy-start.1 = (f32[2048,128,8]{1,0,2:T(8,128)S(1)}, f32[2048,128,8]{1,0,2:T(8,128)}, u32[]{:S(2)}) copy-start(f32[2048,128,8]{1,0,2:T(8,128)} %get-tuple-element.338) | copy-start | bytes 25165828 | tf_op jit(solution)/shard_map/while
  305.1 5.8 %copy-start.1 = (f32[2048,128,8]{1,0,2:T(8,128)S(1)}, f32[2048,128,8]{1,0,2:T(8,128)}, u32[]{:S(2)}) copy-start(f32[2048,128,8]{1,0,2:T(8,128)} %get-tuple-element.338) | copy-start | bytes 25165828 | tf_op jit(solution)/shard_map/while
  319.7 5.8 %copy-start.1 = (f32[2048,128,8]{1,0,2:T(8,128)S(1)}, f32[2048,128,8]{1,0,2:T(8,128)}, u32[]{:S(2)}) copy-start(f32[2048,128,8]{1,0,2:T(8,128)} %get-tuple-element.338) | copy-start | bytes 25165828 | tf_op jit(solution)/shard_map/while
  334.4 5.8 %copy-start.1 = (f32[2048,128,8]{1,0,2:T(8,128)S(1)}, f32[2048,128,8]{1,0,2:T(8,128)}, u32[]{:S(2)}) copy-start(f32[2048,128,8]{1,0,2:T(8,128)} %get-tuple-element.338) | copy-start | bytes 25165828 | tf_op jit(solution)/shard_map/while
Sparse Core Ops, SparseCore 0:
  24.9 115.8 all-gather.3
  145.0 135.4 all-gather.5
where the time goes:
time: 352 us; the launch traced here: 351 us
  waiting for transfers between devices  217 us (62%)
  matrix products  47.4 us (13%)
  other arithmetic  32.7 us (9%)
  local copies, waits for them, and re-layouts  25.8 us (7%)
  blocking collectives  14.2 us (4%)
  between operations  14.2 us (4%)
    all_gather x1, waiting for transfers between devices, body(): piece = lax.all_gather(text_piece, 'ctx', axis=0, tiled=True)  108 us
    all_gather x1, waiting for transfers between devices, body(): piece = lax.all_gather(vision_piece, 'ctx', axis=0, tiled=True)  108 us
    dot_general x6, matrix products, attend(): jnp.einsum('tkgd,skd->tkgs', queries, key_block, preferred_element_type=j...  27.7 us
    reduce_sum x6, other arithmetic, attend(): totals = totals * shrink + jnp.sum(weights, axis=-1)  27.6 us
    dot_general x6, matrix products, attend(): jnp.einsum('tkgs,skd->tkgd', weights.astype(jnp.bfloat16), value_block, p...  19.7 us
    all_to_all x1, blocking collectives, body(): lax.all_to_all(vision_key_value, 'img', split_axis=3, concat_axis=1, tile...  14.2 us
    while x18, local copies, waits for them, and re-layouts  7.15 us
  transfers between devices with their start and end apart: 2, of which 2 were waited for; matrix products, arithmetic and copies ran while one was open for 10% of the time, Pallas kernels for 0%

commit v1 on v0

v1 whole, which is shorter than its diff:
```python
import functools

import jax
import jax.numpy as jnp
from jax import lax
from jax.experimental import pallas as pl
from jax.experimental.pallas import tpu as pltpu
from jax.sharding import PartitionSpec as P

QUERY_HEADS = 64
KEY_VALUE_HEADS = 8
GROUP = QUERY_HEADS // KEY_VALUE_HEADS
HEAD_WIDTH = 128
MBLK = 64
VISION_TOKENS = 64
NEGATIVE = -1e30
SCALE = HEAD_WIDTH**-0.5 * 1.4426950408889634

SIDE = 4
ROWS = 128
PIECE = 2 * ROWS + 2 * VISION_TOKENS
SELF_CHUNKS = 4
CROSS_IMAGES = 8
SELF_ROWS = 256
CROSS_ROWS = 256


def flat(y, x, z, img):
    return ((y * SIDE + x) * SIDE + z) * 8 + img


def all_places():
    return [
        (y, x, z, img)
        for y in range(SIDE)
        for x in range(SIDE)
        for z in range(SIDE)
        for img in range(8)
    ]


def swap_pairs():
    pairs = []
    for y, x, z, img in all_places():
        core = img % 2
        if core != y // 2:
            pairs.append((flat(y, x, z, img), flat(3 - y, x, z, img ^ 1)))
        else:
            pairs.append((flat(y, x, z, img), flat(y, x, z, img)))
    return pairs


def vision_groups():
    return [
        [flat(yy, x, z, img) for yy in (y, 3 - y) for img in range(8)]
        for y in (0, 1)
        for x in range(SIDE)
        for z in range(SIDE)
    ]


def z_groups():
    return [
        [flat(y, x, z, img) for z in range(SIDE)]
        for y in range(SIDE)
        for x in range(SIDE)
        for img in range(8)
    ]


def plane_groups():
    groups = []
    for half in (0, 1):
        for z in range(SIDE):
            for img in range(8):
                core = img % 2
                held = (0, 1) if core == 0 else (2, 3)
                chips = [h if core == half else 3 - h for h in held]
                groups.append([flat(y, x, z, img) for y in chips for x in range(SIDE)])
    return groups


def step(q, keys, values, m_ref, l_ref, acc_ref, rows, visible):
    scores = lax.dot_general(
        q, keys, (((1,), (1,)), ((), ())), preferred_element_type=jnp.float32
    )
    if visible is not None:
        scores = jnp.where(visible, scores, NEGATIVE)
    old = m_ref[rows, :]
    new = jnp.maximum(old, jnp.max(scores, axis=1, keepdims=True))
    weights = jnp.exp2((scores - new[:, :1]) * SCALE)
    if visible is not None:
        weights = jnp.where(visible, weights, 0.0)
    shrink = jnp.exp2((old - new) * SCALE)
    m_ref[rows, :] = new
    l_ref[rows, :] = l_ref[rows, :] * shrink + jnp.sum(weights, axis=1, keepdims=True)
    acc_ref[rows, :] = acc_ref[rows, :] * shrink + jnp.dot(
        weights.astype(jnp.bfloat16), values, preferred_element_type=jnp.float32
    )


def kernel(
    meta, qs_ref, qc_ref, own_ref, other_ref, os_ref, oc_ref, kv, q_ref, m_ref, l_ref, acc_ref, images, sems
):
    row_chunk = meta[1, 2]
    core = row_chunk // 32
    copies = [
        pltpu.make_async_copy(ref, kv.at[pl.ds(32 * (core if i == 0 else 1 - core), 32)], sems.at[i])
        for i, ref in enumerate((own_ref, other_ref))
    ]
    for copy in copies:
        copy.start()

    def reset():
        m_ref[...] = jnp.full_like(m_ref, NEGATIVE)
        l_ref[...] = jnp.zeros_like(l_ref)
        acc_ref[...] = jnp.zeros_like(acc_ref)

    for b in range(2):
        for g in range(GROUP):
            q_ref[b * 512 + g * 64 : b * 512 + g * 64 + 64, :] = qc_ref[
                b * 64 : b * 64 + 64, g * 128 : g * 128 + 128
            ]
    reset()
    counts = []
    for b in range(2):

        def gather(i, count, b=b):
            images[b, count] = i
            return count + meta[0, b * 64 + i]

        counts.append(lax.fori_loop(0, 64, gather, 0, unroll=8))
    for copy in copies:
        copy.wait()
    for b in range(2):
        count = counts[b]
        width = CROSS_IMAGES * VISION_TOKENS

        def block(t, masked, b=b, count=count):
            picks = [
                images[b, jnp.minimum(t * CROSS_IMAGES + u, count - 1)] for u in range(CROSS_IMAGES)
            ]
            keys = jnp.concatenate(
                [kv[i, 2 * ROWS : 2 * ROWS + VISION_TOKENS, :] for i in picks], axis=0
            )
            values = jnp.concatenate(
                [kv[i, 2 * ROWS + VISION_TOKENS : PIECE, :] for i in picks], axis=0
            )
            visible = None
            if masked:
                spot = lax.broadcasted_iota(jnp.int32, (CROSS_ROWS, width), 1)
                visible = spot < (count - t * CROSS_IMAGES) * VISION_TOKENS
            for r in range(0, 512, CROSS_ROWS):
                rows = pl.ds(b * 512 + r, CROSS_ROWS)
                step(q_ref[rows, :], keys, values, m_ref, l_ref, acc_ref, rows, visible)

        full = count // CROSS_IMAGES

        @pl.loop(0, full)
        def _(t, block=block):
            block(t, False)

        @pl.when(full * CROSS_IMAGES < count)
        def _(block=block, full=full):
            block(full, True)

    for b in range(2):
        for g in range(GROUP):
            rows = slice(b * 512 + g * 64, b * 512 + g * 64 + 64)
            oc_ref[b * 64 : b * 64 + 64, g * 128 : g * 128 + 128] = (
                acc_ref[rows, :] / l_ref[rows, :]
            ).astype(jnp.bfloat16)

    for g in range(GROUP):
        q_ref[g * 128 : g * 128 + 128, :] = qs_ref[:, g * 128 : g * 128 + 128]
    reset()
    start0 = meta[1, 0] * MBLK
    start1 = meta[1, 1] * MBLK
    width = SELF_CHUNKS * ROWS
    first = start0 // width
    last = row_chunk // SELF_CHUNKS
    clear = (start1 + width - 1) // width

    def text(t, masked):
        piece = kv[pl.ds(t * SELF_CHUNKS, SELF_CHUNKS), 0 : 2 * ROWS, :]
        keys = piece[:, :ROWS].reshape(width, HEAD_WIDTH)
        values = piece[:, ROWS:].reshape(width, HEAD_WIDTH)
        visible = None
        if masked:
            spot = t * width + lax.broadcasted_iota(jnp.int32, (SELF_ROWS, width), 1)
            row = lax.broadcasted_iota(jnp.int32, (SELF_ROWS, width), 0) % ROWS
            start = jnp.where(row < MBLK, start0, start1)
            visible = (spot <= row_chunk * ROWS + row) & (spot >= start)
        for r in range(0, GROUP * ROWS, SELF_ROWS):
            rows = pl.ds(r, SELF_ROWS)
            step(q_ref[rows, :], keys, values, m_ref, l_ref, acc_ref, rows, visible)

    @pl.loop(first, last + 1)
    def _(t):
        masked = (t == last) | (t < clear)

        @pl.when(masked)
        def _():
            text(t, True)

        @pl.when(jnp.logical_not(masked))
        def _():
            text(t, False)

    for g in range(GROUP):
        rows = slice(g * 128, g * 128 + 128)
        os_ref[:, g * 128 : g * 128 + 128] = (acc_ref[rows, :] / l_ref[rows, :]).astype(jnp.bfloat16)


def attend(meta, self_q, cross_q, own, other):
    whole = pl.BlockSpec(memory_space=pltpu.VMEM)
    anywhere = pl.BlockSpec(memory_space=pl.ANY)
    out = jax.ShapeDtypeStruct((ROWS, GROUP * HEAD_WIDTH), jnp.bfloat16)
    state = pltpu.VMEM((GROUP * ROWS, 128), jnp.float32)
    return pl.pallas_call(
        kernel,
        out_shape=(out, out),
        in_specs=[pl.BlockSpec(memory_space=pltpu.SMEM), whole, whole, anywhere, anywhere],
        out_specs=(whole, whole),
        scratch_shapes=[
            pltpu.VMEM((64, PIECE, HEAD_WIDTH), jnp.bfloat16),
            pltpu.VMEM((GROUP * ROWS, HEAD_WIDTH), jnp.bfloat16),
            state,
            state,
            state,
            pltpu.SMEM((2, 128), jnp.int32),
            pltpu.SemaphoreType.DMA((2,)),
        ],
        compiler_params=pltpu.CompilerParams(vmem_limit_bytes=40 * 1024 * 1024),
        name="attend",
    )(meta, self_q, cross_q, own, other)


AXES = ("ctx", "img")


def body(self_q, text, cross_q, vision, doc_start, image_mask):
    core = lax.axis_index("img") % 2
    swap = functools.partial(lax.ppermute, axis_name=AXES, perm=swap_pairs())

    with jax.named_scope("text_swap"):
        numbers = jnp.concatenate([doc_start // MBLK, lax.axis_index("ctx")[None]])
        meta = jnp.stack([image_mask.reshape(128), jnp.pad(numbers, (0, 125))])
        meta = jnp.pad(meta.astype(jnp.bfloat16), ((0, 14), (0, 0)))
        text = jnp.concatenate([text[:, 0], text[:, 1], meta], axis=0)
        text = swap(text)
        meta = text[2 * ROWS : 2 * ROWS + 2].astype(jnp.int32)

    with jax.named_scope("vision_heads"):
        heads = vision.reshape(8, 2, 4, 2, HEAD_WIDTH).transpose(3, 2, 1, 0, 4)
        heads = jnp.broadcast_to(heads[:, :, None], (2, 4, 2, 2, 8, HEAD_WIDTH))
        heads = lax.all_to_all(
            heads.reshape(16, 16, HEAD_WIDTH), AXES, 0, 0, axis_index_groups=vision_groups(), tiled=True
        )
        heads = lax.dynamic_slice_in_dim(heads, core * 8, 8, 0)
        heads = heads.reshape(8, 2, 8, HEAD_WIDTH).transpose(1, 0, 2, 3).reshape(128, HEAD_WIDTH)

    with jax.named_scope("query_swap"):
        cross_q = swap(cross_q)
        self_q = swap(self_q)

    with jax.named_scope("along_z"):
        piece = jnp.concatenate([text[: 2 * ROWS], heads], axis=0)
        piece = jnp.broadcast_to(piece[None], (4, PIECE, HEAD_WIDTH))
        piece = lax.all_to_all(piece, AXES, 0, 0, axis_index_groups=z_groups(), tiled=True)

    with jax.named_scope("half_plane"):
        piece = jnp.broadcast_to(piece[None], (8, 4, PIECE, HEAD_WIDTH))
        piece = lax.all_to_all(piece, AXES, 0, 0, axis_index_groups=plane_groups(), tiled=True)
        own = piece.reshape(32, PIECE, HEAD_WIDTH)

    with jax.named_scope("cores"):
        other = lax.ppermute(own, "img", [(i, i ^ 1) for i in range(8)])

    with jax.named_scope("attention"):
        self_out, cross_out = attend(meta, self_q, cross_q, own, other)

    with jax.named_scope("return_rows"):
        return swap(self_out), swap(cross_out)


def solution(mesh):
    placed = (
        P("ctx", "img"),
        P("ctx", None, "img"),
        P("ctx", "img"),
        P("ctx", "img", None, None),
        P("ctx"),
        P("ctx", None),
    )
    return jax.shard_map(
        body,
        mesh=mesh,
        in_specs=placed,
        out_specs=(P("ctx", "img"), P("ctx", "img")),
        check_vma=False,
    )
```

time: 352 us -> 169 us (0.48)
  the two profiles are of different devices: /device:TPU:1 before, /device:TPU:35 now
where the time goes in v1:
time: 169 us
  blocking collectives  78.7 us (47%)
  Pallas kernels  41.2 us (24%)
  starting transfers between devices  29.8 us (18%)
  waiting for transfers between devices  12.1 us (7%)
  local copies, waits for them, and re-layouts  4.78 us (3%)
    all_to_all x1, blocking collectives, body(): lax.all_to_all(piece, AXES, 0, 0, axis_index_groups=plane_groups(), tiled...  41.4 us
    pallas_call x1, Pallas kernels, attend(): pl.pallas_call(kernel, out_shape=(out, out), in_specs=[pl.BlockSpec(memor...  41.2 us
    all_to_all x1, blocking collectives, body(): lax.all_to_all(piece, AXES, 0, 0, axis_index_groups=z_groups(), tiled=True)  37.3 us
    all_to_all x1, starting transfers between devices, body(): lax.all_to_all(heads.reshape(16, 16, HEAD_WIDTH), AXES, 0, 0, axis_index_...  8.79 us
    ppermute x2, starting transfers between devices, body(): return (swap(self_out), swap(cross_out))  6.77 us
    ppermute x2, waiting for transfers between devices, body(): return (swap(self_out), swap(cross_out))  4.92 us
    ppermute x1, starting transfers between devices, body(): cross_q = swap(cross_q)  4.85 us
    ppermute x1, starting transfers between devices, body(): text = swap(text)  4.55 us
  transfers between devices with their start and end apart: 7, of which 5 were waited for; matrix products, arithmetic and copies ran while one was open for 2% of the time, Pallas kernels for 0%

profile of v1, /device:TPU:35, one launch (start us, length us, event | category | flops | bytes accessed | tf_op | source)
XLA Modules:
  0.0 168.9 jit_solution(14704046110778960612)
XLA Ops:
  0.6 0.8 reshape.27
  1.4 0.6 broadcast_in_dim.10
  2.1 8.8 %all-to-all-start = ((bf16[16,16,128]{2,1,0:T(8,128)(2,1)}), bf16[16,16,128]{2,1,0:T(8,128)(2,1)S(1)}, u32[]{:S(2)}, u32[]{:S(2)}) async-start(bf16[16,16,128]{2,1,0:T(8,128)(2,1)} %bitcast.5), calls=%async_computation | async-start | bytes 131072 | tf_op jit(solution)/shard_map/vision_heads/all_to_all | solution.py:257
  10.9 0.7 fusion.4
  11.5 0.7 convert.15
  12.2 0.1 reshape.26
  12.3 1.0 fusion.6
  13.3 0.1 fusion.5
  13.5 4.6 %collective-permute-start = (bf16[272,128]{1,0:T(8,128)(2,1)S(1)}, bf16[272,128]{1,0:T(8,128)(2,1)S(1)}, u32[]{:S(2)}, u32[]{:S(2)}) collective-permute-start(bf16[272,128]{1,0:T(8,128)(2,1)S(1)} %pad_maximum_fusion.1), channel_id=1, source_target_pairs={{0,0},{1,384},{2,2},{3,386},{4,4},{5,388},{6,6},{7,390},{8,8},{9,3... | collective-permute-start | bytes 208904 | tf_op jit(solution)/shard_map/text_swap/ppermute | solution.py:251
  18.0 2.3 %collective-permute-done = bf16[272,128]{1,0:T(8,128)(2,1)S(1)} collective-permute-done((bf16[272,128]{1,0:T(8,128)(2,1)S(1)}, bf16[272,128]{1,0:T(8,128)(2,1)S(1)}, u32[]{:S(2)}, u32[]{:S(2)}) %collective-permute-start) | collective-permute-done | bytes 69664 | tf_op jit(solution)/shard_map/text_swap/ppermute | solution.py:251
  20.3 0.0 all-to-all-done
  20.4 0.1 broadcast_in_dim.11
  20.4 37.3 %all_to_all.15 = bf16[4,384,128]{2,1,0:T(8,128)(2,1)S(1)} all-to-all(bf16[4,384,128]{2,1,0:T(8,128)(2,1)S(1)} %broadcast_in_dim.11), channel_id=1, replica_groups={{0,8,16,24},{1,9,17,25},{2,10,18,26},{3,11,19,27},{4,12,20,28},{5,13,21..., dimensions={0} | all-to-all | bytes 786432 | tf_op jit(solution)/shard_map/along_z/all_to_all | solution.py:270
  57.7 0.7 broadcast_in_dim.12
  58.5 0.0 copy-start
  58.5 0.0 copy-start.1
  58.5 41.4 %all_to_all.16 = bf16[8,4,384,128]{3,2,1,0:T(8,128)(2,1)S(1)} all-to-all(bf16[8,4,384,128]{3,2,1,0:T(8,128)(2,1)S(1)} %broadcast_in_dim.12), channel_id=1, replica_groups={{0,32,64,96,128,160,192,224},{129,161,193,225,1,33,65,97},{2,34,66,98,1..., dimensions={0} | all-to-all | bytes 6291456 | tf_op jit(solution)/shard_map/half_plane/all_to_all | solution.py:274
  99.9 2.9 %collective-permute-start.3 = (bf16[32,384,128]{2,1,0:T(8,128)(2,1)S(1)}, bf16[32,384,128]{2,1,0:T(8,128)(2,1)S(1)}, u32[]{:S(2)}, u32[]{:S(2)}) collective-permute-start(bf16[32,384,128]{2,1,0:T(8,128)(2,1)S(1)} %bitcast.15), channel_id=1, source_target_pairs={{0,1},{1,0},{2,3},{3,2},{4,5},{5,4},{6,7},{7,6},{8,9},{9,8},{10,11... | collective-permute-start | bytes 9437192 | tf_op jit(solution)/shard_map/cores/ppermute | solution.py:278
  102.9 0.0 copy-done
  102.9 1.9 %collective-permute-start.1 = (bf16[128,1024]{1,0:T(8,128)(2,1)S(1)}, bf16[128,1024]{1,0:T(8,128)(2,1)S(1)}, u32[]{:S(2)}, u32[]{:S(2)}) collective-permute-start(bf16[128,1024]{1,0:T(8,128)(2,1)S(1)} %copy-done), channel_id=1, source_target_pairs={{0,0},{1,384},{2,2},{3,386},{4,4},{5,388},{6,6},{7,390},{8,8},{9,3... | collective-permute-start | bytes 786440 | tf_op jit(solution)/shard_map/query_swap/ppermute | solution.py:265
  104.8 0.0 copy-done.1
  104.8 4.9 %collective-permute-start.2 = (bf16[128,1024]{1,0:T(8,128)(2,1)S(1)}, bf16[128,1024]{1,0:T(8,128)(2,1)S(1)}, u32[]{:S(2)}, u32[]{:S(2)}) collective-permute-start(bf16[128,1024]{1,0:T(8,128)(2,1)S(1)} %copy-done.1), channel_id=1, source_target_pairs={{0,0},{1,384},{2,2},{3,386},{4,4},{5,388},{6,6},{7,390},{8,8},{9,3... | collective-permute-start | bytes 786440 | tf_op jit(solution)/shard_map/query_swap/ppermute | solution.py:264
  109.7 2.1 %collective-permute-done.1.qs_ref = bf16[128,1024]{1,0:T(8,128)(2,1)S(1)} collective-permute-done((bf16[128,1024]{1,0:T(8,128)(2,1)S(1)}, bf16[128,1024]{1,0:T(8,128)(2,1)S(1)}, u32[]{:S(2)}, u32[]{:S(2)}) %collective-permute-start.1) | collective-permute-done | bytes 262176 | tf_op jit(solution)/shard_map/query_swap/ppermute | solution.py:265
  111.8 2.8 %collective-permute-done.2.qc_ref = bf16[128,1024]{1,0:T(8,128)(2,1)S(1)} collective-permute-done((bf16[128,1024]{1,0:T(8,128)(2,1)S(1)}, bf16[128,1024]{1,0:T(8,128)(2,1)S(1)}, u32[]{:S(2)}, u32[]{:S(2)}) %collective-permute-start.2) | collective-permute-done | bytes 262176 | tf_op jit(solution)/shard_map/query_swap/ppermute | solution.py:264
  114.6 0.0 collective-permute-done.3.other_ref
  114.6 41.2 %attend.1 = (bf16[128,1024]{1,0:T(8,128)(2,1)S(1)}, bf16[128,1024]{1,0:T(8,128)(2,1)S(1)}) custom-call(s32[2,128]{1,0:T(2,128)S(1)} %slice_convert_fusion.meta, bf16[128,1024]{1,0:T(8,128)(2,1)S(1)} %collective-permute-done.1.qs_ref, bf16[128,1024]{1,0:T(8,128)(2,1)S(1)} %collective-permute-done.2.qc_ref, bf16[32,384,128]{2,1,0:T(8,128)(2,1)S(1)} %bitcast.16, ...), custom_call_target="tpu_custom_call" | custom-call | tf_op jit(solution)/shard_map/attention/attend/pallas_call | solution.py:220
  155.8 1.9 %collective-permute-start.4 = (bf16[128,1024]{1,0:T(8,128)(2,1)S(1)}, bf16[128,1024]{1,0:T(8,128)(2,1)S(1)}, u32[]{:S(2)}, u32[]{:S(2)}) collective-permute-start(bf16[128,1024]{1,0:T(8,128)(2,1)S(1)} %get-tuple-element.4), channel_id=1, source_target_pairs={{0,0},{1,384},{2,2},{3,386},{4,4},{5,388},{6,6},{7,390},{8,8},{9,3... | collective-permute-start | bytes 786440 | tf_op jit(solution)/shard_map/return_rows/ppermute | solution.py:284
  157.7 4.9 %collective-permute-start.5 = (bf16[128,1024]{1,0:T(8,128)(2,1)S(1)}, bf16[128,1024]{1,0:T(8,128)(2,1)S(1)}, u32[]{:S(2)}, u32[]{:S(2)}) collective-permute-start(bf16[128,1024]{1,0:T(8,128)(2,1)S(1)} %get-tuple-element.5), channel_id=1, source_target_pairs={{0,0},{1,384},{2,2},{3,386},{4,4},{5,388},{6,6},{7,390},{8,8},{9,3... | collective-permute-start | bytes 786440 | tf_op jit(solution)/shard_map/return_rows/ppermute | solution.py:284
  162.6 2.1 %collective-permute-done.4 = bf16[128,1024]{1,0:T(8,128)(2,1)S(1)} collective-permute-done((bf16[128,1024]{1,0:T(8,128)(2,1)S(1)}, bf16[128,1024]{1,0:T(8,128)(2,1)S(1)}, u32[]{:S(2)}, u32[]{:S(2)}) %collective-permute-start.4) | collective-permute-done | bytes 262176 | tf_op jit(solution)/shard_map/return_rows/ppermute | solution.py:284
  164.7 2.8 %collective-permute-done.5 = bf16[128,1024]{1,0:T(8,128)(2,1)S(1)} collective-permute-done((bf16[128,1024]{1,0:T(8,128)(2,1)S(1)}, bf16[128,1024]{1,0:T(8,128)(2,1)S(1)}, u32[]{:S(2)}, u32[]{:S(2)}) %collective-permute-start.5) | collective-permute-done | bytes 262176 | tf_op jit(solution)/shard_map/return_rows/ppermute | solution.py:284
  167.5 0.7 copy.21
  168.2 0.7 copy.22
  (9 shorter events, 0.1 us)
Async XLA Ops:
  2.1 18.2 %all-to-all-start = ((bf16[16,16,128]{2,1,0:T(8,128)(2,1)}), bf16[16,16,128]{2,1,0:T(8,128)(2,1)S(1)}, u32[]{:S(2)}, u32[]{:S(2)}) async-start(bf16[16,16,128]{2,1,0:T(8,128)(2,1)} %bitcast.5), calls=%async_computation | async-start | bytes 131072 | tf_op jit(solution)/shard_map/vision_heads/all_to_all | solution.py:257
  13.5 6.8 %collective-permute-start = (bf16[272,128]{1,0:T(8,128)(2,1)S(1)}, bf16[272,128]{1,0:T(8,128)(2,1)S(1)}, u32[]{:S(2)}, u32[]{:S(2)}) collective-permute-start(bf16[272,128]{1,0:T(8,128)(2,1)S(1)} %pad_maximum_fusion.1), channel_id=1, source_target_pairs={{0,0},{1,384},{2,2},{3,386},{4,4},{5,388},{6,6},{7,390},{8,8},{9,3... | collective-permute-start | bytes 208904 | tf_op jit(solution)/shard_map/text_swap/ppermute | solution.py:251
  58.5 44.4 %copy-start = (bf16[128,1024]{1,0:T(8,128)(2,1)S(1)}, bf16[128,1024]{1,0:T(8,128)(2,1)}, u32[]{:S(2)}) copy-start(bf16[128,1024]{1,0:T(8,128)(2,1)} %param.6) | copy-start | bytes 786436
  58.5 46.3 %copy-start.1 = (bf16[128,1024]{1,0:T(8,128)(2,1)S(1)}, bf16[128,1024]{1,0:T(8,128)(2,1)}, u32[]{:S(2)}) copy-start(bf16[128,1024]{1,0:T(8,128)(2,1)} %param.8) | copy-start | bytes 786436
  99.9 14.7 %collective-permute-start.3 = (bf16[32,384,128]{2,1,0:T(8,128)(2,1)S(1)}, bf16[32,384,128]{2,1,0:T(8,128)(2,1)S(1)}, u32[]{:S(2)}, u32[]{:S(2)}) collective-permute-start(bf16[32,384,128]{2,1,0:T(8,128)(2,1)S(1)} %bitcast.15), channel_id=1, source_target_pairs={{0,1},{1,0},{2,3},{3,2},{4,5},{5,4},{6,7},{7,6},{8,9},{9,8},{10,11... | collective-permute-start | bytes 9437192 | tf_op jit(solution)/shard_map/cores/ppermute | solution.py:278
  102.9 8.9 %collective-permute-start.1 = (bf16[128,1024]{1,0:T(8,128)(2,1)S(1)}, bf16[128,1024]{1,0:T(8,128)(2,1)S(1)}, u32[]{:S(2)}, u32[]{:S(2)}) collective-permute-start(bf16[128,1024]{1,0:T(8,128)(2,1)S(1)} %copy-done), channel_id=1, source_target_pairs={{0,0},{1,384},{2,2},{3,386},{4,4},{5,388},{6,6},{7,390},{8,8},{9,3... | collective-permute-start | bytes 786440 | tf_op jit(solution)/shard_map/query_swap/ppermute | solution.py:265
  104.8 9.8 %collective-permute-start.2 = (bf16[128,1024]{1,0:T(8,128)(2,1)S(1)}, bf16[128,1024]{1,0:T(8,128)(2,1)S(1)}, u32[]{:S(2)}, u32[]{:S(2)}) collective-permute-start(bf16[128,1024]{1,0:T(8,128)(2,1)S(1)} %copy-done.1), channel_id=1, source_target_pairs={{0,0},{1,384},{2,2},{3,386},{4,4},{5,388},{6,6},{7,390},{8,8},{9,3... | collective-permute-start | bytes 786440 | tf_op jit(solution)/shard_map/query_swap/ppermute | solution.py:264
  155.8 8.9 %collective-permute-start.4 = (bf16[128,1024]{1,0:T(8,128)(2,1)S(1)}, bf16[128,1024]{1,0:T(8,128)(2,1)S(1)}, u32[]{:S(2)}, u32[]{:S(2)}) collective-permute-start(bf16[128,1024]{1,0:T(8,128)(2,1)S(1)} %get-tuple-element.4), channel_id=1, source_target_pairs={{0,0},{1,384},{2,2},{3,386},{4,4},{5,388},{6,6},{7,390},{8,8},{9,3... | collective-permute-start | bytes 786440 | tf_op jit(solution)/shard_map/return_rows/ppermute | solution.py:284
  157.7 9.8 %collective-permute-start.5 = (bf16[128,1024]{1,0:T(8,128)(2,1)S(1)}, bf16[128,1024]{1,0:T(8,128)(2,1)S(1)}, u32[]{:S(2)}, u32[]{:S(2)}) collective-permute-start(bf16[128,1024]{1,0:T(8,128)(2,1)S(1)} %get-tuple-element.5), channel_id=1, source_target_pairs={{0,0},{1,384},{2,2},{3,386},{4,4},{5,388},{6,6},{7,390},{8,8},{9,3... | collective-permute-start | bytes 786440 | tf_op jit(solution)/shard_map/return_rows/ppermute | solution.py:284

commit v2 on v1

v2 whole, which is shorter than its diff:
```python
import functools

import jax
import jax.numpy as jnp
from jax import lax
from jax.experimental import pallas as pl
from jax.experimental.pallas import tpu as pltpu
from jax.sharding import PartitionSpec as P

QUERY_HEADS = 64
KEY_VALUE_HEADS = 8
GROUP = QUERY_HEADS // KEY_VALUE_HEADS
HEAD_WIDTH = 128
MBLK = 64
VISION_TOKENS = 64
NEGATIVE = -1e30
SCALE = HEAD_WIDTH**-0.5 * 1.4426950408889634

SIDE = 4
ROWS = 128
TEXT = 2 * ROWS
VISION = 2 * VISION_TOKENS
SELF_CHUNKS = 4
SELF_ROWS = 256
CROSS_ROWS = 256


def flat(y, x, z, img):
    return ((y * SIDE + x) * SIDE + z) * 8 + img


def all_places():
    return [
        (y, x, z, img)
        for y in range(SIDE)
        for x in range(SIDE)
        for z in range(SIDE)
        for img in range(8)
    ]


def swap_pairs():
    pairs = []
    for y, x, z, img in all_places():
        core = img % 2
        if core != y // 2:
            pairs.append((flat(y, x, z, img), flat(3 - y, x, z, img ^ 1)))
        else:
            pairs.append((flat(y, x, z, img), flat(y, x, z, img)))
    return pairs


def vision_groups():
    return [
        [flat(yy, x, z, img) for yy in (y, 3 - y) for img in range(8)]
        for y in (0, 1)
        for x in range(SIDE)
        for z in range(SIDE)
    ]


def z_groups():
    return [
        [flat(y, x, z, img) for z in range(SIDE)]
        for y in range(SIDE)
        for x in range(SIDE)
        for img in range(8)
    ]


def plane_groups():
    groups = []
    for half in (0, 1):
        for z in range(SIDE):
            for img in range(8):
                core = img % 2
                held = (0, 1) if core == 0 else (2, 3)
                chips = [h if core == half else 3 - h for h in held]
                groups.append([flat(y, x, z, img) for y in chips for x in range(SIDE)])
    return groups


def scores_of(q, keys, visible):
    scores = lax.dot_general(
        q, keys, (((1,), (1,)), ((), ())), preferred_element_type=jnp.float32
    )
    return scores if visible is None else jnp.where(visible, scores, NEGATIVE)


def mix(scores, shift, values, visible):
    shift = jnp.concatenate([shift] * (scores.shape[1] // 128), axis=1)
    weights = jnp.exp2((scores - shift) * SCALE)
    if visible is not None:
        weights = jnp.where(visible, weights, 0.0)
    both = jnp.concatenate([values, jnp.ones_like(values)], axis=1)
    return jnp.dot(weights.astype(jnp.bfloat16), both, preferred_element_type=jnp.float32)


def first_step(q, keys, values, m_ref, acc_ref, rows, visible):
    scores = scores_of(q, keys, visible)
    top = jnp.broadcast_to(jnp.max(scores, axis=1, keepdims=True), (scores.shape[0], 128))
    m_ref[rows, :] = top
    acc_ref[rows, :] = mix(scores, top, values, visible)


def quick_step(q, keys, values, m_ref, acc_ref, rows, visible):
    scores = scores_of(q, keys, visible)
    acc_ref[rows, :] += mix(scores, m_ref[rows, :], values, visible)


def careful_step(q, keys, values, m_ref, acc_ref, rows, visible):
    scores = scores_of(q, keys, visible)
    old = m_ref[rows, :]
    new = jnp.maximum(old, jnp.max(scores, axis=1, keepdims=True))
    shrink = jnp.exp2((old - new) * SCALE)
    m_ref[rows, :] = new
    acc_ref[rows, :] = acc_ref[rows, :] * jnp.concatenate([shrink, shrink], axis=1) + mix(
        scores, new, values, visible
    )


def steady(acc_ref):
    return jnp.all(acc_ref[:, 128:] < 2.0**100)


def reset(m_ref, acc_ref):
    m_ref[...] = jnp.full_like(m_ref, NEGATIVE)
    acc_ref[...] = jnp.zeros_like(acc_ref)


def cross(meta, core, q_ref, own_ref, other_ref, m_ref, acc_ref, images):
    counts = []
    for b in range(2):
        for part, half in ((0, core), (1, 1 - core)):

            def gather(i, count, b=b, part=part, half=half):
                images[2 * b + part, count] = (i & ~3) | ((meta[0, 65] - i) & 3)
                return count + meta[b, 32 * half + i]

            counts.append(lax.fori_loop(0, 32, gather, 0, unroll=8))

    def load(b, part, start, number):
        ref = (own_ref, other_ref)[part]
        top = jnp.maximum(counts[2 * b + part] - 1, 0)
        picks = [images[2 * b + part, jnp.minimum(start + u, top)] for u in range(number)]
        keys = [ref[i, :VISION_TOKENS, :] for i in picks]
        values = [ref[i, VISION_TOKENS:, :] for i in picks]
        return keys, values

    def run(one_step, b, keys, values, visible):
        keys = jnp.concatenate(keys, axis=0)
        values = jnp.concatenate(values, axis=0)
        for r in range(0, 512, CROSS_ROWS):
            rows = pl.ds(b * 512 + r, CROSS_ROWS)
            one_step(q_ref[rows, :], keys, values, m_ref, acc_ref, rows, visible)

    def sweep(b, begin, later):
        groups = [jnp.maximum(counts[2 * b + part] - 1, 0) // 4 for part in range(2)]
        tails = [counts[2 * b + part] - groups[part] * 4 for part in range(2)]
        keys, values = [], []
        for part in range(2):
            k, v = load(b, part, groups[part] * 4, 4)
            keys += k
            values += v
        width = 4 * VISION_TOKENS
        spot = lax.broadcasted_iota(jnp.int32, (CROSS_ROWS, 2 * width), 1)
        visible = (spot < tails[0] * VISION_TOKENS) | (
            (spot >= width) & (spot < width + tails[1] * VISION_TOKENS)
        )
        run(begin, b, keys, values, visible)
        for part in range(2):
            pairs = groups[part] // 2

            @pl.loop(0, pairs)
            def _(t, part=part):
                run(later, b, *load(b, part, t * 8, 8), None)

            @pl.when(groups[part] % 2 == 1)
            def _(part=part, pairs=pairs):
                run(later, b, *load(b, part, pairs * 8, 4), None)

    for b in range(2):
        sweep(b, first_step, quick_step)

    @pl.when(jnp.logical_not(steady(acc_ref)))
    def _():
        reset(m_ref, acc_ref)
        for b in range(2):
            sweep(b, careful_step, careful_step)


def self_attention(meta, core, q_ref, own_ref, other_ref, m_ref, acc_ref):
    start0 = meta[0, 64] * MBLK
    start1 = meta[1, 64] * MBLK
    row_chunk = meta[0, 65]
    width = SELF_CHUNKS * ROWS
    tiles = 32 // SELF_CHUNKS
    first = start0 // width
    last = row_chunk // SELF_CHUNKS
    clear = (start1 + width - 1) // width

    def tile(one_step, ref, base, t, number, masked):
        keys_wide = number * width
        piece = ref[pl.ds((t - base) * SELF_CHUNKS, number * SELF_CHUNKS), :, :]
        keys = piece[:, :ROWS].reshape(keys_wide, HEAD_WIDTH)
        values = piece[:, ROWS:].reshape(keys_wide, HEAD_WIDTH)
        visible = None
        if masked:
            spot = lax.broadcasted_iota(jnp.int32, (SELF_ROWS, keys_wide), 1)
            spot = t * width + ((row_chunk - spot // ROWS) & 3) * ROWS + spot % ROWS
            row = lax.broadcasted_iota(jnp.int32, (SELF_ROWS, keys_wide), 0) % ROWS
            start = jnp.where(row < MBLK, start0, start1)
            visible = (spot <= row_chunk * ROWS + row) & (spot >= start)
        for r in range(0, GROUP * ROWS, SELF_ROWS):
            rows = pl.ds(r, SELF_ROWS)
            one_step(q_ref[rows, :], keys, values, m_ref, acc_ref, rows, visible)

    def sweep(begin, later):
        tile(begin, own_ref, core * tiles, last, 1, True)
        for ref, half, stop in ((own_ref, core, last), (other_ref, 0, core * tiles)):
            base = half * tiles
            low = jnp.maximum(first, base)
            stop = jnp.maximum(stop, low)
            edge = jnp.clip(clear, low, stop)
            odd = (stop - edge) % 2

            @pl.loop(low, edge)
            def _(t, ref=ref, base=base):
                tile(later, ref, base, t, 1, True)

            @pl.when(odd == 1)
            def _(ref=ref, base=base, edge=edge):
                tile(later, ref, base, edge, 1, False)

            @pl.loop(0, (stop - edge) // 2)
            def _(p, ref=ref, base=base, from_tile=edge + odd):
                tile(later, ref, base, from_tile + 2 * p, 2, False)

    sweep(first_step, quick_step)

    @pl.when(jnp.logical_not(steady(acc_ref)))
    def _():
        reset(m_ref, acc_ref)
        sweep(careful_step, careful_step)


def cross_kernel(meta, q_in, own_ref, other_ref, out_ref, q_ref, m_ref, acc_ref, images):
    places = [(b, g, b * 512 + g * MBLK) for b in range(2) for g in range(GROUP)]
    for b, g, row in places:
        q_ref[row : row + MBLK, :] = q_in[b * MBLK : b * MBLK + MBLK, g * 128 : g * 128 + 128]
    cross(meta, meta[0, 65] // 32, q_ref, own_ref, other_ref, m_ref, acc_ref, images)
    for b, g, row in places:
        rows = slice(row, row + MBLK)
        out_ref[b * MBLK : b * MBLK + MBLK, g * 128 : g * 128 + 128] = (
            acc_ref[rows, :128] / acc_ref[rows, 128:]
        ).astype(jnp.bfloat16)


def self_kernel(meta, q_in, own_ref, other_ref, out_ref, q_ref, m_ref, acc_ref):
    for g in range(GROUP):
        q_ref[g * 128 : g * 128 + 128, :] = q_in[:, g * 128 : g * 128 + 128]
    self_attention(meta, meta[0, 65] // 32, q_ref, own_ref, other_ref, m_ref, acc_ref)
    for g in range(GROUP):
        rows = slice(g * 128, g * 128 + 128)
        out_ref[:, g * 128 : g * 128 + 128] = (acc_ref[rows, :128] / acc_ref[rows, 128:]).astype(
            jnp.bfloat16
        )


def attend(kernel, name, keys, meta, queries, own, other):
    whole = pl.BlockSpec(memory_space=pltpu.VMEM)
    scratch = [
        pltpu.VMEM((GROUP * ROWS, HEAD_WIDTH), jnp.bfloat16),
        pltpu.VMEM((GROUP * ROWS, 128), jnp.float32),
        pltpu.VMEM((GROUP * ROWS, 256), jnp.float32),
    ]
    if kernel is cross_kernel:
        scratch.append(pltpu.SMEM((4, 128), jnp.int32))
    return pl.pallas_call(
        kernel,
        out_shape=jax.ShapeDtypeStruct((ROWS, GROUP * HEAD_WIDTH), jnp.bfloat16),
        in_specs=[pl.BlockSpec(memory_space=pltpu.SMEM), whole, whole, whole],
        out_specs=whole,
        scratch_shapes=scratch,
        compiler_params=pltpu.CompilerParams(vmem_limit_bytes=28 * 1024 * 1024),
        cost_estimate=pl.CostEstimate(
            flops=8 * GROUP * ROWS * keys * HEAD_WIDTH,
            bytes_accessed=4 * keys * HEAD_WIDTH + 4 * GROUP * ROWS * HEAD_WIDTH,
            transcendentals=GROUP * ROWS * keys,
        ),
        name=name,
    )(meta, queries, own, other)


AXES = ("ctx", "img")


def body(self_q, text, cross_q, vision, doc_start, image_mask):
    core = lax.axis_index("img") % 2
    swap = functools.partial(lax.ppermute, axis_name=AXES, perm=swap_pairs())

    with jax.named_scope("text_swap"):
        place = jnp.full((2, 1), lax.axis_index("ctx"), jnp.int32)
        meta = jnp.concatenate([image_mask, (doc_start // MBLK)[:, None], place], axis=1)
        meta = jnp.pad(meta.astype(jnp.bfloat16), ((0, 14), (0, 62)))
        text = jnp.concatenate([text[:, 0], text[:, 1], meta], axis=0)
        heads = vision.reshape(8, 2, 4, 2, HEAD_WIDTH).transpose(3, 2, 1, 0, 4)
        heads = jnp.broadcast_to(heads[:, :, None], (2, 4, 2, 2, 8, HEAD_WIDTH))
        text, heads = lax.optimization_barrier((text, heads))
        text = swap(text)

    def along_z(part):
        pieces = [part]
        for k in range(1, SIDE):
            steps = [
                (flat(y, x, z, img), flat(y, x, (z + k) % SIDE, img)) for y, x, z, img in all_places()
            ]
            pieces.append(lax.ppermute(part, AXES, steps))
        return pieces

    def half_plane(pieces):
        part = jnp.stack(pieces)
        part = jnp.broadcast_to(part[None], (8,) + part.shape)
        part = lax.all_to_all(part, AXES, 0, 0, axis_index_groups=plane_groups(), tiled=True)
        return part.reshape((32,) + part.shape[2:])

    def cores(part):
        return lax.ppermute(part, "img", [(i, i ^ 1) for i in range(8)])

    with jax.named_scope("text_z"):
        text_z = along_z(text[:TEXT])
        meta = text[TEXT : TEXT + 2].astype(jnp.int32)

    with jax.named_scope("vision_heads"):
        heads = lax.all_to_all(
            heads.reshape(16, 16, HEAD_WIDTH), AXES, 0, 0, axis_index_groups=vision_groups(), tiled=True
        )

    with jax.named_scope("query_swap"):
        cross_q = swap(cross_q)
        self_q = swap(self_q)

    text_z, heads, self_q, cross_q = lax.optimization_barrier((text_z, heads, self_q, cross_q))

    with jax.named_scope("vision_z"):
        heads = lax.dynamic_slice_in_dim(heads, core * 8, 8, 0)
        heads = heads.reshape(8, 2, 8, HEAD_WIDTH).transpose(1, 0, 2, 3).reshape(128, HEAD_WIDTH)
        vision_z = along_z(heads)

    with jax.named_scope("text_plane"):
        own_text = half_plane(text_z)

    own_text, vision_z = lax.optimization_barrier((own_text, vision_z))

    with jax.named_scope("vision_plane"):
        own_vision = half_plane(vision_z)

    with jax.named_scope("self_attention"):
        other_text = cores(own_text)
        self_out = attend(self_kernel, "self_attention", 8192, meta, self_q, own_text, other_text)

    self_out, own_vision = lax.optimization_barrier((self_out, own_vision))

    with jax.named_scope("cross_attention"):
        other_vision = cores(own_vision)
        cross_out = attend(
            cross_kernel, "cross_attention", 4096, meta, cross_q, own_vision, other_vision
        )
    return swap(self_out), swap(cross_out)


def solution(mesh):
    placed = (
        P("ctx", "img"),
        P("ctx", None, "img"),
        P("ctx", "img"),
        P("ctx", "img", None, None),
        P("ctx"),
        P("ctx", None),
    )
    return jax.shard_map(
        body,
        mesh=mesh,
        in_specs=placed,
        out_specs=(P("ctx", "img"), P("ctx", "img")),
        check_vma=False,
    )
```

time: 169 us -> 146 us (0.86)
  the two profiles are of different devices: /device:TPU:35 before, /device:TPU:71 now
where the time goes in v2:
time: 146 us; the launch traced here: 145 us
  starting transfers between devices  80.7 us (55%)
  waiting for transfers between devices  27.7 us (19%)
  Pallas kernels  25.3 us (17%)
  local copies, waits for them, and re-layouts  8.76 us (6%)
  other arithmetic  1.5 us (1%)
    ppermute x6, starting transfers between devices, along_z(): pieces.append(lax.ppermute(part, AXES, steps))  37 us
    pallas_call x2, Pallas kernels, attend(): pl.pallas_call(kernel, out_shape=jax.ShapeDtypeStruct((ROWS, GROUP * HEAD...  25.3 us
    ppermute x6, waiting for transfers between devices, along_z(): pieces.append(lax.ppermute(part, AXES, steps))  12.3 us
    all_to_all x2, starting transfers between devices, half_plane(): lax.all_to_all(part, AXES, 0, 0, axis_index_groups=plane_groups(), tiled=...  10.5 us
    ppermute x2, starting transfers between devices, body(): return (swap(self_out), swap(cross_out))  8.71 us
    all_to_all x1, starting transfers between devices, body(): lax.all_to_all(heads.reshape(16, 16, HEAD_WIDTH), AXES, 0, 0, axis_index_...  7.98 us
    ppermute x2, waiting for transfers between devices, body(): return (swap(self_out), swap(cross_out))  6.97 us
    all_to_all x2, waiting for transfers between devices, half_plane(): lax.all_to_all(part, AXES, 0, 0, axis_index_groups=plane_groups(), tiled=...  6.14 us
  transfers between devices with their start and end apart: 16, of which 7 were waited for; matrix products, arithmetic and copies ran while one was open for 4% of the time, Pallas kernels for 17%

profile of v2, /device:TPU:71, one launch (start us, length us, event | category | flops | bytes accessed | tf_op | source)
XLA Modules:
  0.0 144.8 jit_solution(8185385803357748741)
XLA Ops:
  0.6 5.2 %collective-permute-start.4 = (bf16[128,1024]{1,0:T(8,128)(2,1)}, bf16[128,1024]{1,0:T(8,128)(2,1)S(1)}, u32[]{:S(2)}, u32[]{:S(2)}) collective-permute-start(bf16[128,1024]{1,0:T(8,128)(2,1)} %param.6), channel_id=1, source_target_pairs={{0,0},{1,384},{2,2},{3,386},{4,4},{5,388},{6,6},{7,390},{8,8},{9,3... | collective-permute-start | bytes 786440 | tf_op jit(solution)/shard_map/query_swap/ppermute | solution.py:341
  5.8 1.9 %collective-permute-start.5 = (bf16[128,1024]{1,0:T(8,128)(2,1)}, bf16[128,1024]{1,0:T(8,128)(2,1)S(1)}, u32[]{:S(2)}, u32[]{:S(2)}) collective-permute-start(bf16[128,1024]{1,0:T(8,128)(2,1)} %param.8), channel_id=1, source_target_pairs={{0,0},{1,384},{2,2},{3,386},{4,4},{5,388},{6,6},{7,390},{8,8},{9,3... | collective-permute-start | bytes 786440 | tf_op jit(solution)/shard_map/query_swap/ppermute | solution.py:340
  9.2 1.0 fusion.2
  10.4 0.8 reshape.25
  11.9 8.0 %all-to-all-start = ((bf16[16,16,128]{2,1,0:T(8,128)(2,1)}), bf16[16,16,128]{2,1,0:T(8,128)(2,1)S(1)}, u32[]{:S(2)}, u32[]{:S(2)}) async-start(bf16[16,16,128]{2,1,0:T(8,128)(2,1)} %bitcast.4), calls=%async_computation | async-start | bytes 131072 | tf_op jit(solution)/shard_map/vision_heads/all_to_all | solution.py:335
  19.9 4.5 %collective-permute-start = (bf16[272,128]{1,0:T(8,128)(2,1)S(1)}, bf16[272,128]{1,0:T(8,128)(2,1)S(1)}, u32[]{:S(2)}, u32[]{:S(2)}) collective-permute-start(bf16[272,128]{1,0:T(8,128)(2,1)S(1)} %fusion.1), channel_id=1, source_target_pairs={{0,0},{1,384},{2,2},{3,386},{4,4},{5,388},{6,6},{7,390},{8,8},{9,3... | collective-permute-start | bytes 208904 | tf_op jit(solution)/shard_map/text_swap/ppermute | solution.py:310
  24.4 2.3 %collective-permute-done = bf16[272,128]{1,0:T(8,128)(2,1)S(1)} collective-permute-done((bf16[272,128]{1,0:T(8,128)(2,1)S(1)}, bf16[272,128]{1,0:T(8,128)(2,1)S(1)}, u32[]{:S(2)}, u32[]{:S(2)}) %collective-permute-start) | collective-permute-done | bytes 69664 | tf_op jit(solution)/shard_map/text_swap/ppermute | solution.py:310
  26.7 8.8 %collective-permute-start.1 = (bf16[256,128]{1,0:T(8,128)(2,1)S(1)}, bf16[256,128]{1,0:T(8,128)(2,1)S(1)}, u32[]{:S(2)}, u32[]{:S(2)}) collective-permute-start(bf16[256,128]{1,0:T(8,128)(2,1)S(1)} %slice.17), channel_id=1, source_target_pairs={{0,8},{1,9},{2,10},{3,11},{4,12},{5,13},{6,14},{7,15},{8,16},{9,17... | collective-permute-start | bytes 196616 | tf_op jit(solution)/shard_map/text_z/ppermute | solution.py:318
  35.5 7.9 %collective-permute-start.2 = (bf16[256,128]{1,0:T(8,128)(2,1)S(1)}, bf16[256,128]{1,0:T(8,128)(2,1)S(1)}, u32[]{:S(2)}, u32[]{:S(2)}) collective-permute-start(bf16[256,128]{1,0:T(8,128)(2,1)S(1)} %slice.17), channel_id=1, source_target_pairs={{0,16},{1,17},{2,18},{3,19},{4,20},{5,21},{6,22},{7,23},{8,24},{9,... | collective-permute-start | bytes 196616 | tf_op jit(solution)/shard_map/text_z/ppermute | solution.py:318
  43.5 5.2 %collective-permute-start.3 = (bf16[256,128]{1,0:T(8,128)(2,1)S(1)}, bf16[256,128]{1,0:T(8,128)(2,1)S(1)}, u32[]{:S(2)}, u32[]{:S(2)}) collective-permute-start(bf16[256,128]{1,0:T(8,128)(2,1)S(1)} %slice.17), channel_id=1, source_target_pairs={{0,24},{1,25},{2,26},{3,27},{4,28},{5,29},{6,30},{7,31},{8,0},{9,1... | collective-permute-start | bytes 196616 | tf_op jit(solution)/shard_map/text_z/ppermute | solution.py:318
  48.7 1.6 %collective-permute-done.2 = bf16[256,128]{1,0:T(8,128)(2,1)S(1)} collective-permute-done((bf16[256,128]{1,0:T(8,128)(2,1)S(1)}, bf16[256,128]{1,0:T(8,128)(2,1)S(1)}, u32[]{:S(2)}, u32[]{:S(2)}) %collective-permute-start.2) | collective-permute-done | bytes 65568 | tf_op jit(solution)/shard_map/text_z/ppermute | solution.py:318
  50.3 4.1 %collective-permute-done.3 = bf16[256,128]{1,0:T(8,128)(2,1)S(1)} collective-permute-done((bf16[256,128]{1,0:T(8,128)(2,1)S(1)}, bf16[256,128]{1,0:T(8,128)(2,1)S(1)}, u32[]{:S(2)}, u32[]{:S(2)}) %collective-permute-start.3) | collective-permute-done | bytes 65568 | tf_op jit(solution)/shard_map/text_z/ppermute | solution.py:318
  54.4 1.8 %broadcast_in_dim.28 = bf16[8,4,256,128]{3,2,1,0:T(8,128)(2,1)} broadcast(bf16[4,256,128]{2,1,0:T(8,128)(2,1)S(1)} %pad_maximum_fusion), dimensions={1,2,3} | broadcast | bytes 2359296 | tf_op jit(solution)/shard_map/text_plane/broadcast_in_dim | solution.py:323
  56.2 5.1 %all-to-all-start.1 = ((bf16[8,4,256,128]{3,2,1,0:T(8,128)(2,1)}), bf16[8,4,256,128]{3,2,1,0:T(8,128)(2,1)S(1)}, u32[]{:S(2)}, u32[]{:S(2)}) async-start(bf16[8,4,256,128]{3,2,1,0:T(8,128)(2,1)} %broadcast_in_dim.28), calls=%async_computation.1 | async-start | bytes 4194304 | tf_op jit(solution)/shard_map/text_plane/all_to_all | solution.py:324
  61.3 3.6 %collective-permute-start.6 = (bf16[128,128]{1,0:T(8,128)(2,1)S(1)}, bf16[128,128]{1,0:T(8,128)(2,1)S(1)}, u32[]{:S(2)}, u32[]{:S(2)}) collective-permute-start(bf16[128,128]{1,0:T(8,128)(2,1)S(1)} %bitcast.30), channel_id=1, source_target_pairs={{0,8},{1,9},{2,10},{3,11},{4,12},{5,13},{6,14},{7,15},{8,16},{9,17... | collective-permute-start | bytes 98312 | tf_op jit(solution)/shard_map/vision_z/ppermute | solution.py:318
  64.9 8.3 %collective-permute-start.7 = (bf16[128,128]{1,0:T(8,128)(2,1)S(1)}, bf16[128,128]{1,0:T(8,128)(2,1)S(1)}, u32[]{:S(2)}, u32[]{:S(2)}) collective-permute-start(bf16[128,128]{1,0:T(8,128)(2,1)S(1)} %bitcast.31), channel_id=1, source_target_pairs={{0,16},{1,17},{2,18},{3,19},{4,20},{5,21},{6,22},{7,23},{8,24},{9,... | collective-permute-start | bytes 98312 | tf_op jit(solution)/shard_map/vision_z/ppermute | solution.py:318
  73.2 3.2 %collective-permute-start.8 = (bf16[128,128]{1,0:T(8,128)(2,1)S(1)}, bf16[128,128]{1,0:T(8,128)(2,1)S(1)}, u32[]{:S(2)}, u32[]{:S(2)}) collective-permute-start(bf16[128,128]{1,0:T(8,128)(2,1)S(1)} %bitcast.32), channel_id=1, source_target_pairs={{0,24},{1,25},{2,26},{3,27},{4,28},{5,29},{6,30},{7,31},{8,0},{9,1... | collective-permute-start | bytes 98312 | tf_op jit(solution)/shard_map/vision_z/ppermute | solution.py:318
  76.4 2.2 %collective-permute-done.7 = bf16[128,128]{1,0:T(8,128)(2,1)S(1)} collective-permute-done((bf16[128,128]{1,0:T(8,128)(2,1)S(1)}, bf16[128,128]{1,0:T(8,128)(2,1)S(1)}, u32[]{:S(2)}, u32[]{:S(2)}) %collective-permute-start.7) | collective-permute-done | bytes 32800 | tf_op jit(solution)/shard_map/vision_z/ppermute | solution.py:318
  78.7 4.5 %collective-permute-done.8 = bf16[128,128]{1,0:T(8,128)(2,1)S(1)} collective-permute-done((bf16[128,128]{1,0:T(8,128)(2,1)S(1)}, bf16[128,128]{1,0:T(8,128)(2,1)S(1)}, u32[]{:S(2)}, u32[]{:S(2)}) %collective-permute-start.8) | collective-permute-done | bytes 32800 | tf_op jit(solution)/shard_map/vision_z/ppermute | solution.py:318
  83.1 1.9 %collective-permute-start.9 = (bf16[32,256,128]{2,1,0:T(8,128)(2,1)S(1)}, bf16[32,256,128]{2,1,0:T(8,128)(2,1)}, u32[]{:S(2)}, u32[]{:S(2)}) collective-permute-start(bf16[32,256,128]{2,1,0:T(8,128)(2,1)S(1)} %bitcast.24), channel_id=1, source_target_pairs={{0,1},{1,0},{2,3},{3,2},{4,5},{5,4},{6,7},{7,6},{8,9},{9,8},{10,11... | collective-permute-start | bytes 6291464 | tf_op jit(solution)/shard_map/self_attention/ppermute | solution.py:328
  85.1 1.2 broadcast_in_dim.29
  86.3 5.4 %all-to-all-start.2 = ((bf16[8,4,128,128]{3,2,1,0:T(8,128)(2,1)}), bf16[8,4,128,128]{3,2,1,0:T(8,128)(2,1)S(1)}, u32[]{:S(2)}, u32[]{:S(2)}) async-start(bf16[8,4,128,128]{3,2,1,0:T(8,128)(2,1)} %broadcast_in_dim.29), calls=%async_computation.2 | async-start | bytes 2097152 | tf_op jit(solution)/shard_map/vision_plane/all_to_all | solution.py:324
  91.7 0.9 copy-done.1
  92.6 5.4 %self_attention.1 = bf16[128,1024]{1,0:T(8,128)(2,1)S(1)} custom-call(s32[2,128]{1,0:T(2,128)S(1)} %slice_convert_fusion.meta, bf16[128,1024]{1,0:T(8,128)(2,1)S(1)} %copy-done.1, bf16[32,256,128]{2,1,0:T(8,128)(2,1)S(1)} %bitcast.25, bf16[32,256,128]{2,1,0:T(8,128)(2,1)} %collective-permute-done.9.other_ref), custom_call_target="tpu_custom_call" | custom-call | flops 8589934592 | bytes 4718592 | tf_op jit(solution)/shard_map/self_attention/self_attention/pallas_call | solution.py:279
  98.8 6.1 %all-to-all-done.2 = bf16[8,4,128,128]{3,2,1,0:T(8,128)(2,1)S(1)} async-done(((bf16[8,4,128,128]{3,2,1,0:T(8,128)(2,1)}), bf16[8,4,128,128]{3,2,1,0:T(8,128)(2,1)S(1)}, u32[]{:S(2)}, u32[]{:S(2)}) %all-to-all-start.2) | async-done | bytes 1048608 | tf_op jit(solution)/shard_map/vision_plane/all_to_all | solution.py:324
  104.9 3.0 %collective-permute-start.11 = (bf16[32,128,128]{2,1,0:T(8,128)(2,1)S(1)}, bf16[32,128,128]{2,1,0:T(8,128)(2,1)S(1)}, u32[]{:S(2)}, u32[]{:S(2)}) collective-permute-start(bf16[32,128,128]{2,1,0:T(8,128)(2,1)S(1)} %bitcast.26), channel_id=1, source_target_pairs={{0,1},{1,0},{2,3},{3,2},{4,5},{5,4},{6,7},{7,6},{8,9},{9,8},{10,11... | collective-permute-start | bytes 3145736 | tf_op jit(solution)/shard_map/cross_attention/ppermute | solution.py:328
  107.9 6.8 %collective-permute-start.10 = (bf16[128,1024]{1,0:T(8,128)(2,1)}, bf16[128,1024]{1,0:T(8,128)(2,1)S(1)}, u32[]{:S(2)}, u32[]{:S(2)}) collective-permute-start(bf16[128,1024]{1,0:T(8,128)(2,1)} %copy-done.2), channel_id=1, source_target_pairs={{0,0},{1,384},{2,2},{3,386},{4,4},{5,388},{6,6},{7,390},{8,8},{9,3... | collective-permute-start | bytes 786440 | tf_op jit(solution)/shard_map/ppermute | solution.py:369
  114.7 19.8 %cross_attention.1 = bf16[128,1024]{1,0:T(8,128)(2,1)S(1)} custom-call(s32[2,128]{1,0:T(2,128)S(1)} %slice_convert_fusion.meta, bf16[128,1024]{1,0:T(8,128)(2,1)S(1)} %collective-permute-done.5.q_in, bf16[32,128,128]{2,1,0:T(8,128)(2,1)S(1)} %bitcast.27, bf16[32,128,128]{2,1,0:T(8,128)(2,1)S(1)} %collective-permute-done.11.other_ref), custom_call_target="tpu_custom_call" | custom-call | flops 4294967296 | bytes 2621440 | tf_op jit(solution)/shard_map/cross_attention/cross_attention/pallas_call | solution.py:279
  134.5 1.9 %collective-permute-start.12 = (bf16[128,1024]{1,0:T(8,128)(2,1)S(1)}, bf16[128,1024]{1,0:T(8,128)(2,1)S(1)}, u32[]{:S(2)}, u32[]{:S(2)}) collective-permute-start(bf16[128,1024]{1,0:T(8,128)(2,1)S(1)} %cross_attention.1), channel_id=1, source_target_pairs={{0,0},{1,384},{2,2},{3,386},{4,4},{5,388},{6,6},{7,390},{8,8},{9,3... | collective-permute-start | bytes 786440 | tf_op jit(solution)/shard_map/ppermute | solution.py:369
  136.5 7.0 %collective-permute-done.12 = bf16[128,1024]{1,0:T(8,128)(2,1)S(1)} collective-permute-done((bf16[128,1024]{1,0:T(8,128)(2,1)S(1)}, bf16[128,1024]{1,0:T(8,128)(2,1)S(1)}, u32[]{:S(2)}, u32[]{:S(2)}) %collective-permute-start.12) | collective-permute-done | bytes 262176 | tf_op jit(solution)/shard_map/ppermute | solution.py:369
  143.4 0.7 copy.27
  144.1 0.7 copy.28
  (29 shorter events, 3.1 us)
Async XLA Ops:
  0.6 53.7 %collective-permute-start.4 = (bf16[128,1024]{1,0:T(8,128)(2,1)}, bf16[128,1024]{1,0:T(8,128)(2,1)S(1)}, u32[]{:S(2)}, u32[]{:S(2)}) collective-permute-start(bf16[128,1024]{1,0:T(8,128)(2,1)} %param.6), channel_id=1, source_target_pairs={{0,0},{1,384},{2,2},{3,386},{4,4},{5,388},{6,6},{7,390},{8,8},{9,3... | collective-permute-start | bytes 786440 | tf_op jit(solution)/shard_map/query_swap/ppermute | solution.py:341
  5.8 48.5 %collective-permute-start.5 = (bf16[128,1024]{1,0:T(8,128)(2,1)}, bf16[128,1024]{1,0:T(8,128)(2,1)S(1)}, u32[]{:S(2)}, u32[]{:S(2)}) collective-permute-start(bf16[128,1024]{1,0:T(8,128)(2,1)} %param.8), channel_id=1, source_target_pairs={{0,0},{1,384},{2,2},{3,386},{4,4},{5,388},{6,6},{7,390},{8,8},{9,3... | collective-permute-start | bytes 786440 | tf_op jit(solution)/shard_map/query_swap/ppermute | solution.py:340
  11.9 42.4 %all-to-all-start = ((bf16[16,16,128]{2,1,0:T(8,128)(2,1)}), bf16[16,16,128]{2,1,0:T(8,128)(2,1)S(1)}, u32[]{:S(2)}, u32[]{:S(2)}) async-start(bf16[16,16,128]{2,1,0:T(8,128)(2,1)} %bitcast.4), calls=%async_computation | async-start | bytes 131072 | tf_op jit(solution)/shard_map/vision_heads/all_to_all | solution.py:335
  19.9 6.8 %collective-permute-start = (bf16[272,128]{1,0:T(8,128)(2,1)S(1)}, bf16[272,128]{1,0:T(8,128)(2,1)S(1)}, u32[]{:S(2)}, u32[]{:S(2)}) collective-permute-start(bf16[272,128]{1,0:T(8,128)(2,1)S(1)} %fusion.1), channel_id=1, source_target_pairs={{0,0},{1,384},{2,2},{3,386},{4,4},{5,388},{6,6},{7,390},{8,8},{9,3... | collective-permute-start | bytes 208904 | tf_op jit(solution)/shard_map/text_swap/ppermute | solution.py:310
  26.7 22.0 %collective-permute-start.1 = (bf16[256,128]{1,0:T(8,128)(2,1)S(1)}, bf16[256,128]{1,0:T(8,128)(2,1)S(1)}, u32[]{:S(2)}, u32[]{:S(2)}) collective-permute-start(bf16[256,128]{1,0:T(8,128)(2,1)S(1)} %slice.17), channel_id=1, source_target_pairs={{0,8},{1,9},{2,10},{3,11},{4,12},{5,13},{6,14},{7,15},{8,16},{9,17... | collective-permute-start | bytes 196616 | tf_op jit(solution)/shard_map/text_z/ppermute | solution.py:318
  35.5 14.7 %collective-permute-start.2 = (bf16[256,128]{1,0:T(8,128)(2,1)S(1)}, bf16[256,128]{1,0:T(8,128)(2,1)S(1)}, u32[]{:S(2)}, u32[]{:S(2)}) collective-permute-start(bf16[256,128]{1,0:T(8,128)(2,1)S(1)} %slice.17), channel_id=1, source_target_pairs={{0,16},{1,17},{2,18},{3,19},{4,20},{5,21},{6,22},{7,23},{8,24},{9,... | collective-permute-start | bytes 196616 | tf_op jit(solution)/shard_map/text_z/ppermute | solution.py:318
  43.5 10.9 %collective-permute-start.3 = (bf16[256,128]{1,0:T(8,128)(2,1)S(1)}, bf16[256,128]{1,0:T(8,128)(2,1)S(1)}, u32[]{:S(2)}, u32[]{:S(2)}) collective-permute-start(bf16[256,128]{1,0:T(8,128)(2,1)S(1)} %slice.17), channel_id=1, source_target_pairs={{0,24},{1,25},{2,26},{3,27},{4,28},{5,29},{6,30},{7,31},{8,0},{9,1... | collective-permute-start | bytes 196616 | tf_op jit(solution)/shard_map/text_z/ppermute | solution.py:318
  54.3 1.9 %copy-start = (bf16[128,1024]{1,0:T(8,128)(2,1)}, bf16[128,1024]{1,0:T(8,128)(2,1)S(1)}, u32[]{:S(2)}) copy-start(bf16[128,1024]{1,0:T(8,128)(2,1)S(1)} %collective-permute-done.4.q_in) | copy-start | bytes 786436
  56.2 26.9 %all-to-all-start.1 = ((bf16[8,4,256,128]{3,2,1,0:T(8,128)(2,1)}), bf16[8,4,256,128]{3,2,1,0:T(8,128)(2,1)S(1)}, u32[]{:S(2)}, u32[]{:S(2)}) async-start(bf16[8,4,256,128]{3,2,1,0:T(8,128)(2,1)} %broadcast_in_dim.28), calls=%async_computation.1 | async-start | bytes 4194304 | tf_op jit(solution)/shard_map/text_plane/all_to_all | solution.py:324
  61.3 15.1 %collective-permute-start.6 = (bf16[128,128]{1,0:T(8,128)(2,1)S(1)}, bf16[128,128]{1,0:T(8,128)(2,1)S(1)}, u32[]{:S(2)}, u32[]{:S(2)}) collective-permute-start(bf16[128,128]{1,0:T(8,128)(2,1)S(1)} %bitcast.30), channel_id=1, source_target_pairs={{0,8},{1,9},{2,10},{3,11},{4,12},{5,13},{6,14},{7,15},{8,16},{9,17... | collective-permute-start | bytes 98312 | tf_op jit(solution)/shard_map/vision_z/ppermute | solution.py:318
  64.9 13.7 %collective-permute-start.7 = (bf16[128,128]{1,0:T(8,128)(2,1)S(1)}, bf16[128,128]{1,0:T(8,128)(2,1)S(1)}, u32[]{:S(2)}, u32[]{:S(2)}) collective-permute-start(bf16[128,128]{1,0:T(8,128)(2,1)S(1)} %bitcast.31), channel_id=1, source_target_pairs={{0,16},{1,17},{2,18},{3,19},{4,20},{5,21},{6,22},{7,23},{8,24},{9,... | collective-permute-start | bytes 98312 | tf_op jit(solution)/shard_map/vision_z/ppermute | solution.py:318
  73.2 9.9 %collective-permute-start.8 = (bf16[128,128]{1,0:T(8,128)(2,1)S(1)}, bf16[128,128]{1,0:T(8,128)(2,1)S(1)}, u32[]{:S(2)}, u32[]{:S(2)}) collective-permute-start(bf16[128,128]{1,0:T(8,128)(2,1)S(1)} %bitcast.32), channel_id=1, source_target_pairs={{0,24},{1,25},{2,26},{3,27},{4,28},{5,29},{6,30},{7,31},{8,0},{9,1... | collective-permute-start | bytes 98312 | tf_op jit(solution)/shard_map/vision_z/ppermute | solution.py:318
  83.1 8.6 %collective-permute-start.9 = (bf16[32,256,128]{2,1,0:T(8,128)(2,1)S(1)}, bf16[32,256,128]{2,1,0:T(8,128)(2,1)}, u32[]{:S(2)}, u32[]{:S(2)}) collective-permute-start(bf16[32,256,128]{2,1,0:T(8,128)(2,1)S(1)} %bitcast.24), channel_id=1, source_target_pairs={{0,1},{1,0},{2,3},{3,2},{4,5},{5,4},{6,7},{7,6},{8,9},{9,8},{10,11... | collective-permute-start | bytes 6291464 | tf_op jit(solution)/shard_map/self_attention/ppermute | solution.py:328
  86.3 18.6 %all-to-all-start.2 = ((bf16[8,4,128,128]{3,2,1,0:T(8,128)(2,1)}), bf16[8,4,128,128]{3,2,1,0:T(8,128)(2,1)S(1)}, u32[]{:S(2)}, u32[]{:S(2)}) async-start(bf16[8,4,128,128]{3,2,1,0:T(8,128)(2,1)} %broadcast_in_dim.29), calls=%async_computation.2 | async-start | bytes 2097152 | tf_op jit(solution)/shard_map/vision_plane/all_to_all | solution.py:324
  91.7 1.0 copy-start.1
  98.1 0.7 copy-start.2
  104.9 9.8 %collective-permute-start.11 = (bf16[32,128,128]{2,1,0:T(8,128)(2,1)S(1)}, bf16[32,128,128]{2,1,0:T(8,128)(2,1)S(1)}, u32[]{:S(2)}, u32[]{:S(2)}) collective-permute-start(bf16[32,128,128]{2,1,0:T(8,128)(2,1)S(1)} %bitcast.26), channel_id=1, source_target_pairs={{0,1},{1,0},{2,3},{3,2},{4,5},{5,4},{6,7},{7,6},{8,9},{9,8},{10,11... | collective-permute-start | bytes 3145736 | tf_op jit(solution)/shard_map/cross_attention/ppermute | solution.py:328
  107.9 28.6 %collective-permute-start.10 = (bf16[128,1024]{1,0:T(8,128)(2,1)}, bf16[128,1024]{1,0:T(8,128)(2,1)S(1)}, u32[]{:S(2)}, u32[]{:S(2)}) collective-permute-start(bf16[128,1024]{1,0:T(8,128)(2,1)} %copy-done.2), channel_id=1, source_target_pairs={{0,0},{1,384},{2,2},{3,386},{4,4},{5,388},{6,6},{7,390},{8,8},{9,3... | collective-permute-start | bytes 786440 | tf_op jit(solution)/shard_map/ppermute | solution.py:369
  134.5 8.9 %collective-permute-start.12 = (bf16[128,1024]{1,0:T(8,128)(2,1)S(1)}, bf16[128,1024]{1,0:T(8,128)(2,1)S(1)}, u32[]{:S(2)}, u32[]{:S(2)}) collective-permute-start(bf16[128,1024]{1,0:T(8,128)(2,1)S(1)} %cross_attention.1), channel_id=1, source_target_pairs={{0,0},{1,384},{2,2},{3,386},{4,4},{5,388},{6,6},{7,390},{8,8},{9,3... | collective-permute-start | bytes 786440 | tf_op jit(solution)/shard_map/ppermute | solution.py:369

commit v3 on v2

--- a/solution.py
+++ b/solution.py
@@ -134,7 +134,7 @@
         for part, half in ((0, core), (1, 1 - core)):
 
             def gather(i, count, b=b, part=part, half=half):
-                images[2 * b + part, count] = (i & ~3) | ((meta[0, 65] - i) & 3)
+                images[2 * b + part, count] = i
                 return count + meta[b, 32 * half + i]
 
             counts.append(lax.fori_loop(0, 32, gather, 0, unroll=8))
@@ -206,8 +206,7 @@
         values = piece[:, ROWS:].reshape(keys_wide, HEAD_WIDTH)
         visible = None
         if masked:
-            spot = lax.broadcasted_iota(jnp.int32, (SELF_ROWS, keys_wide), 1)
-            spot = t * width + ((row_chunk - spot // ROWS) & 3) * ROWS + spot % ROWS
+            spot = t * width + lax.broadcasted_iota(jnp.int32, (SELF_ROWS, keys_wide), 1)
             row = lax.broadcasted_iota(jnp.int32, (SELF_ROWS, keys_wide), 0) % ROWS
             start = jnp.where(row < MBLK, start0, start1)
             visible = (spot <= row_chunk * ROWS + row) & (spot >= start)
@@ -247,7 +246,9 @@
 def cross_kernel(meta, q_in, own_ref, other_ref, out_ref, q_ref, m_ref, acc_ref, images):
     places = [(b, g, b * 512 + g * MBLK) for b in range(2) for g in range(GROUP)]
     for b, g, row in places:
-        q_ref[row : row + MBLK, :] = q_in[b * MBLK : b * MBLK + MBLK, g * 128 : g * 128 + 128]
+        q_ref[row : row + MBLK, :] = q_in[
+            ROWS + b * MBLK : ROWS + b * MBLK + MBLK, g * 128 : g * 128 + 128
+        ]
     cross(meta, meta[0, 65] // 32, q_ref, own_ref, other_ref, m_ref, acc_ref, images)
     for b, g, row in places:
         rows = slice(row, row + MBLK)
@@ -258,7 +259,7 @@
 
 def self_kernel(meta, q_in, own_ref, other_ref, out_ref, q_ref, m_ref, acc_ref):
     for g in range(GROUP):
-        q_ref[g * 128 : g * 128 + 128, :] = q_in[:, g * 128 : g * 128 + 128]
+        q_ref[g * 128 : g * 128 + 128, :] = q_in[:ROWS, g * 128 : g * 128 + 128]
     self_attention(meta, meta[0, 65] // 32, q_ref, own_ref, other_ref, m_ref, acc_ref)
     for g in range(GROUP):
         rows = slice(g * 128, g * 128 + 128)
@@ -304,22 +305,13 @@
         meta = jnp.concatenate([image_mask, (doc_start // MBLK)[:, None], place], axis=1)
         meta = jnp.pad(meta.astype(jnp.bfloat16), ((0, 14), (0, 62)))
         text = jnp.concatenate([text[:, 0], text[:, 1], meta], axis=0)
-        heads = vision.reshape(8, 2, 4, 2, HEAD_WIDTH).transpose(3, 2, 1, 0, 4)
-        heads = jnp.broadcast_to(heads[:, :, None], (2, 4, 2, 2, 8, HEAD_WIDTH))
-        text, heads = lax.optimization_barrier((text, heads))
         text = swap(text)
 
     def along_z(part):
-        pieces = [part]
-        for k in range(1, SIDE):
-            steps = [
-                (flat(y, x, z, img), flat(y, x, (z + k) % SIDE, img)) for y, x, z, img in all_places()
-            ]
-            pieces.append(lax.ppermute(part, AXES, steps))
-        return pieces
-
-    def half_plane(pieces):
-        part = jnp.stack(pieces)
+        part = jnp.broadcast_to(part[None], (SIDE,) + part.shape)
+        return lax.all_to_all(part, AXES, 0, 0, axis_index_groups=z_groups(), tiled=True)
+
+    def half_plane(part):
         part = jnp.broadcast_to(part[None], (8,) + part.shape)
         part = lax.all_to_all(part, AXES, 0, 0, axis_index_groups=plane_groups(), tiled=True)
         return part.reshape((32,) + part.shape[2:])
@@ -327,44 +319,43 @@
     def cores(part):
         return lax.ppermute(part, "img", [(i, i ^ 1) for i in range(8)])
 
-    with jax.named_scope("text_z"):
-        text_z = along_z(text[:TEXT])
-        meta = text[TEXT : TEXT + 2].astype(jnp.int32)
-
     with jax.named_scope("vision_heads"):
+        heads = vision.reshape(8, 2, 4, 2, HEAD_WIDTH).transpose(3, 2, 1, 0, 4)
+        heads = jnp.broadcast_to(heads[:, :, None], (2, 4, 2, 2, 8, HEAD_WIDTH))
         heads = lax.all_to_all(
             heads.reshape(16, 16, HEAD_WIDTH), AXES, 0, 0, axis_index_groups=vision_groups(), tiled=True
         )
-
-    with jax.named_scope("query_swap"):
-        cross_q = swap(cross_q)
-        self_q = swap(self_q)
-
-    text_z, heads, self_q, cross_q = lax.optimization_barrier((text_z, heads, self_q, cross_q))
-
-    with jax.named_scope("vision_z"):
         heads = lax.dynamic_slice_in_dim(heads, core * 8, 8, 0)
         heads = heads.reshape(8, 2, 8, HEAD_WIDTH).transpose(1, 0, 2, 3).reshape(128, HEAD_WIDTH)
-        vision_z = along_z(heads)
+
+    with jax.named_scope("query_swap"):
+        queries = swap(jnp.concatenate([self_q, cross_q], axis=0))
+
+    text, heads, queries = lax.optimization_barrier((text, heads, queries))
+    meta = text[TEXT : TEXT + 2].astype(jnp.int32)
+
+    with jax.named_scope("along_z"):
+        piece = along_z(jnp.concatenate([text[:TEXT], heads], axis=0))
 
     with jax.named_scope("text_plane"):
-        own_text = half_plane(text_z)
-
-    own_text, vision_z = lax.optimization_barrier((own_text, vision_z))
+        own_text = half_plane(piece[:, :TEXT])
+
+    own_text, piece = lax.optimization_barrier((own_text, piece))
+    vision_z = piece[:, TEXT:]
 
     with jax.named_scope("vision_plane"):
         own_vision = half_plane(vision_z)
 
     with jax.named_scope("self_attention"):
         other_text = cores(own_text)
-        self_out = attend(self_kernel, "self_attention", 8192, meta, self_q, own_text, other_text)
+        self_out = attend(self_kernel, "self_attention", 8192, meta, queries, own_text, other_text)
 
     self_out, own_vision = lax.optimization_barrier((self_out, own_vision))
 
     with jax.named_scope("cross_attention"):
         other_vision = cores(own_vision)
         cross_out = attend(
-            cross_kernel, "cross_attention", 4096, meta, cross_q, own_vision, other_vision
+            cross_kernel, "cross_attention", 4096, meta, queries, own_vision, other_vision
         )
     return swap(self_out), swap(cross_out)
 

time: 146 us -> 141 us (0.966)
  the two profiles are of different devices: /device:TPU:71 before, /device:TPU:35 now
where the time goes in v3:
time: 141 us; the launch traced here: 139 us
  blocking collectives  56.1 us (40%)
  starting transfers between devices  29 us (21%)
  Pallas kernels  24.5 us (17%)
  waiting for transfers between devices  18.4 us (13%)
  local copies, waits for them, and re-layouts  7.93 us (6%)
  other arithmetic  2.51 us (2%)
    all_to_all x1, blocking collectives, along_z(): lax.all_to_all(part, AXES, 0, 0, axis_index_groups=z_groups(), tiled=True)  30.2 us
    all_to_all x1, blocking collectives, half_plane(): lax.all_to_all(part, AXES, 0, 0, axis_index_groups=plane_groups(), tiled=...  25.9 us
    pallas_call x2, Pallas kernels, attend(): pl.pallas_call(kernel, out_shape=jax.ShapeDtypeStruct((ROWS, GROUP * HEAD...  24.5 us
    all_to_all x1, starting transfers between devices, body(): lax.all_to_all(heads.reshape(16, 16, HEAD_WIDTH), AXES, 0, 0, axis_index_...  8.79 us
    ppermute x2, waiting for transfers between devices, body(): return (swap(self_out), swap(cross_out))  6.88 us
    all_to_all x1, waiting for transfers between devices, half_plane(): lax.all_to_all(part, AXES, 0, 0, axis_index_groups=plane_groups(), tiled=...  6.64 us
    ppermute x2, starting transfers between devices, cores(): return lax.ppermute(part, 'img', [(i, i ^ 1) for i in range(8)])  5.21 us
    ppermute x1, waiting for transfers between devices, body(): text = swap(text)  4.55 us
  transfers between devices with their start and end apart: 8, of which 4 were waited for; matrix products, arithmetic and copies ran while one was open for 4% of the time, Pallas kernels for 18%

profile of v3, /device:TPU:35, one launch (start us, length us, event | category | flops | bytes accessed | tf_op | source)
XLA Modules:
  0.0 139.3 jit_solution(15635948043545956281)
XLA Ops:
  0.6 0.8 reshape.26
  1.4 0.6 broadcast_in_dim.15
  2.1 8.8 %all-to-all-start = ((bf16[16,16,128]{2,1,0:T(8,128)(2,1)}), bf16[16,16,128]{2,1,0:T(8,128)(2,1)S(1)}, u32[]{:S(2)}, u32[]{:S(2)}) async-start(bf16[16,16,128]{2,1,0:T(8,128)(2,1)} %bitcast.4), calls=%async_computation | async-start | bytes 131072 | tf_op jit(solution)/shard_map/vision_heads/all_to_all | solution.py:325
  10.9 1.1 pad_maximum_fusion
  11.9 4.6 %collective-permute-start.1 = (bf16[256,1024]{1,0:T(8,128)(2,1)S(1)}, bf16[256,1024]{1,0:T(8,128)(2,1)S(1)}, u32[]{:S(2)}, u32[]{:S(2)}) collective-permute-start(bf16[256,1024]{1,0:T(8,128)(2,1)S(1)} %pad_maximum_fusion), channel_id=1, source_target_pairs={{0,0},{1,384},{2,2},{3,386},{4,4},{5,388},{6,6},{7,390},{8,8},{9,3... | collective-permute-start | bytes 1572872 | tf_op jit(solution)/shard_map/query_swap/ppermute | solution.py:332
  16.5 1.0 fusion.2
  17.5 0.7 convert_bitcast_fusion
  18.2 0.1 copy.14
  18.3 0.7 convert.11
  19.0 0.1 pad.14.clone
  19.1 0.1 maximum_maximum_fusion
  19.2 2.2 %collective-permute-start = (bf16[272,128]{1,0:T(8,128)(2,1)S(1)}, bf16[272,128]{1,0:T(8,128)(2,1)S(1)}, u32[]{:S(2)}, u32[]{:S(2)}) collective-permute-start(bf16[272,128]{1,0:T(8,128)(2,1)S(1)} %fusion.1), channel_id=1, source_target_pairs={{0,0},{1,384},{2,2},{3,386},{4,4},{5,388},{6,6},{7,390},{8,8},{9,3... | collective-permute-start | bytes 208904 | tf_op jit(solution)/shard_map/text_swap/ppermute | solution.py:308
  21.4 4.6 %collective-permute-done = bf16[272,128]{1,0:T(8,128)(2,1)S(1)} collective-permute-done((bf16[272,128]{1,0:T(8,128)(2,1)S(1)}, bf16[272,128]{1,0:T(8,128)(2,1)S(1)}, u32[]{:S(2)}, u32[]{:S(2)}) %collective-permute-start) | collective-permute-done | bytes 69664 | tf_op jit(solution)/shard_map/text_swap/ppermute | solution.py:308
  26.0 0.1 broadcast_in_dim.16
  26.1 30.2 %all_to_all.20 = bf16[4,384,128]{2,1,0:T(8,128)(2,1)S(1)} all-to-all(bf16[4,384,128]{2,1,0:T(8,128)(2,1)S(1)} %broadcast_in_dim.16), channel_id=1, replica_groups={{0,8,16,24},{1,9,17,25},{2,10,18,26},{3,11,19,27},{4,12,20,28},{5,13,21..., dimensions={0} | all-to-all | bytes 786432 | tf_op jit(solution)/shard_map/along_z/all_to_all | solution.py:312
  56.3 0.5 broadcast_in_dim.17
  56.8 25.9 %all_to_all.21 = bf16[8,4,256,128]{3,2,1,0:T(8,128)(2,1)S(1)} all-to-all(bf16[8,4,256,128]{3,2,1,0:T(8,128)(2,1)S(1)} %broadcast_in_dim.17), channel_id=1, replica_groups={{0,32,64,96,128,160,192,224},{129,161,193,225,1,33,65,97},{2,34,66,98,1..., dimensions={0} | all-to-all | bytes 4194304 | tf_op jit(solution)/shard_map/text_plane/all_to_all | solution.py:316
  82.7 1.9 %collective-permute-start.2 = (bf16[32,256,128]{2,1,0:T(8,128)(2,1)S(1)}, bf16[32,256,128]{2,1,0:T(8,128)(2,1)}, u32[]{:S(2)}, u32[]{:S(2)}) collective-permute-start(bf16[32,256,128]{2,1,0:T(8,128)(2,1)S(1)} %bitcast.16), channel_id=1, source_target_pairs={{0,1},{1,0},{2,3},{3,2},{4,5},{5,4},{6,7},{7,6},{8,9},{9,8},{10,11... | collective-permute-start | bytes 6291464 | tf_op jit(solution)/shard_map/self_attention/ppermute | solution.py:320
  84.6 1.2 broadcast_in_dim.36
  85.8 4.3 %all-to-all-start.3 = ((bf16[8,4,128,128]{3,2,1,0:T(8,128)(2,1)}), bf16[8,4,128,128]{3,2,1,0:T(8,128)(2,1)S(1)}, u32[]{:S(2)}, u32[]{:S(2)}) async-start(bf16[8,4,128,128]{3,2,1,0:T(8,128)(2,1)} %broadcast_in_dim.36), calls=%async_computation.3 | async-start | bytes 2097152 | tf_op jit(solution)/shard_map/vision_plane/all_to_all | solution.py:316
  90.2 1.0 copy-done.1
  91.2 5.8 %self_attention.1 = bf16[128,1024]{1,0:T(8,128)(2,1)S(1)} custom-call(s32[2,128]{1,0:T(2,128)S(1)} %slice_convert_fusion.meta, bf16[256,1024]{1,0:T(8,128)(2,1)S(1)} %copy-done.1, bf16[32,256,128]{2,1,0:T(8,128)(2,1)S(1)} %bitcast.17, bf16[32,256,128]{2,1,0:T(8,128)(2,1)} %collective-permute-done.2.other_ref), custom_call_target="tpu_custom_call" | custom-call | flops 8589934592 | bytes 4718592 | tf_op jit(solution)/shard_map/self_attention/self_attention/pallas_call | solution.py:280
  97.0 6.6 %all-to-all-done.3 = bf16[8,4,128,128]{3,2,1,0:T(8,128)(2,1)S(1)} async-done(((bf16[8,4,128,128]{3,2,1,0:T(8,128)(2,1)}), bf16[8,4,128,128]{3,2,1,0:T(8,128)(2,1)S(1)}, u32[]{:S(2)}, u32[]{:S(2)}) %all-to-all-start.3) | async-done | bytes 1048608 | tf_op jit(solution)/shard_map/vision_plane/all_to_all | solution.py:316
  103.6 3.3 %collective-permute-start.4 = (bf16[32,128,128]{2,1,0:T(8,128)(2,1)S(1)}, bf16[32,128,128]{2,1,0:T(8,128)(2,1)S(1)}, u32[]{:S(2)}, u32[]{:S(2)}) collective-permute-start(bf16[32,128,128]{2,1,0:T(8,128)(2,1)S(1)} %bitcast.18), channel_id=1, source_target_pairs={{0,1},{1,0},{2,3},{3,2},{4,5},{5,4},{6,7},{7,6},{8,9},{9,8},{10,11... | collective-permute-start | bytes 3145736 | tf_op jit(solution)/shard_map/cross_attention/ppermute | solution.py:320
  106.9 1.9 %collective-permute-start.3 = (bf16[128,1024]{1,0:T(8,128)(2,1)S(1)}, bf16[128,1024]{1,0:T(8,128)(2,1)S(1)}, u32[]{:S(2)}, u32[]{:S(2)}) collective-permute-start(bf16[128,1024]{1,0:T(8,128)(2,1)S(1)} %self_attention.1), channel_id=1, source_target_pairs={{0,0},{1,384},{2,2},{3,386},{4,4},{5,388},{6,6},{7,390},{8,8},{9,3... | collective-permute-start | bytes 786440 | tf_op jit(solution)/shard_map/ppermute | solution.py:360
  108.8 0.3 collective-permute-done.4.other_ref
  109.2 1.0 copy-done.2
  110.2 18.8 %cross_attention.1 = bf16[128,1024]{1,0:T(8,128)(2,1)S(1)} custom-call(s32[2,128]{1,0:T(2,128)S(1)} %slice_convert_fusion.meta, bf16[256,1024]{1,0:T(8,128)(2,1)S(1)} %copy-done.2, bf16[32,128,128]{2,1,0:T(8,128)(2,1)S(1)} %bitcast.19, bf16[32,128,128]{2,1,0:T(8,128)(2,1)S(1)} %collective-permute-done.4.other_ref), custom_call_target="tpu_custom_call" | custom-call | flops 4294967296 | bytes 2621440 | tf_op jit(solution)/shard_map/cross_attention/cross_attention/pallas_call | solution.py:280
  129.0 2.0 %collective-permute-start.5 = (bf16[128,1024]{1,0:T(8,128)(2,1)S(1)}, bf16[128,1024]{1,0:T(8,128)(2,1)S(1)}, u32[]{:S(2)}, u32[]{:S(2)}) collective-permute-start(bf16[128,1024]{1,0:T(8,128)(2,1)S(1)} %cross_attention.1), channel_id=1, source_target_pairs={{0,0},{1,384},{2,2},{3,386},{4,4},{5,388},{6,6},{7,390},{8,8},{9,3... | collective-permute-start | bytes 786440 | tf_op jit(solution)/shard_map/ppermute | solution.py:360
  131.0 6.9 %collective-permute-done.5 = bf16[128,1024]{1,0:T(8,128)(2,1)S(1)} collective-permute-done((bf16[128,1024]{1,0:T(8,128)(2,1)S(1)}, bf16[128,1024]{1,0:T(8,128)(2,1)S(1)}, u32[]{:S(2)}, u32[]{:S(2)}) %collective-permute-start.5) | collective-permute-done | bytes 262176 | tf_op jit(solution)/shard_map/ppermute | solution.py:360
  137.9 0.7 copy.23
  138.6 0.7 copy.24
  (18 shorter events, 0.1 us)
Async XLA Ops:
  2.1 19.3 %all-to-all-start = ((bf16[16,16,128]{2,1,0:T(8,128)(2,1)}), bf16[16,16,128]{2,1,0:T(8,128)(2,1)S(1)}, u32[]{:S(2)}, u32[]{:S(2)}) async-start(bf16[16,16,128]{2,1,0:T(8,128)(2,1)} %bitcast.4), calls=%async_computation | async-start | bytes 131072 | tf_op jit(solution)/shard_map/vision_heads/all_to_all | solution.py:325
  11.9 14.1 %collective-permute-start.1 = (bf16[256,1024]{1,0:T(8,128)(2,1)S(1)}, bf16[256,1024]{1,0:T(8,128)(2,1)S(1)}, u32[]{:S(2)}, u32[]{:S(2)}) collective-permute-start(bf16[256,1024]{1,0:T(8,128)(2,1)S(1)} %pad_maximum_fusion), channel_id=1, source_target_pairs={{0,0},{1,384},{2,2},{3,386},{4,4},{5,388},{6,6},{7,390},{8,8},{9,3... | collective-permute-start | bytes 1572872 | tf_op jit(solution)/shard_map/query_swap/ppermute | solution.py:332
  19.2 6.8 %collective-permute-start = (bf16[272,128]{1,0:T(8,128)(2,1)S(1)}, bf16[272,128]{1,0:T(8,128)(2,1)S(1)}, u32[]{:S(2)}, u32[]{:S(2)}) collective-permute-start(bf16[272,128]{1,0:T(8,128)(2,1)S(1)} %fusion.1), channel_id=1, source_target_pairs={{0,0},{1,384},{2,2},{3,386},{4,4},{5,388},{6,6},{7,390},{8,8},{9,3... | collective-permute-start | bytes 208904 | tf_op jit(solution)/shard_map/text_swap/ppermute | solution.py:308
  26.0 30.3 %copy-start = (bf16[256,1024]{1,0:T(8,128)(2,1)}, bf16[256,1024]{1,0:T(8,128)(2,1)S(1)}, u32[]{:S(2)}) copy-start(bf16[256,1024]{1,0:T(8,128)(2,1)S(1)} %collective-permute-done.1.q_in) | copy-start | bytes 1572868
  82.7 7.5 %collective-permute-start.2 = (bf16[32,256,128]{2,1,0:T(8,128)(2,1)S(1)}, bf16[32,256,128]{2,1,0:T(8,128)(2,1)}, u32[]{:S(2)}, u32[]{:S(2)}) collective-permute-start(bf16[32,256,128]{2,1,0:T(8,128)(2,1)S(1)} %bitcast.16), channel_id=1, source_target_pairs={{0,1},{1,0},{2,3},{3,2},{4,5},{5,4},{6,7},{7,6},{8,9},{9,8},{10,11... | collective-permute-start | bytes 6291464 | tf_op jit(solution)/shard_map/self_attention/ppermute | solution.py:320
  85.8 17.8 %all-to-all-start.3 = ((bf16[8,4,128,128]{3,2,1,0:T(8,128)(2,1)}), bf16[8,4,128,128]{3,2,1,0:T(8,128)(2,1)S(1)}, u32[]{:S(2)}, u32[]{:S(2)}) async-start(bf16[8,4,128,128]{3,2,1,0:T(8,128)(2,1)} %broadcast_in_dim.36), calls=%async_computation.3 | async-start | bytes 2097152 | tf_op jit(solution)/shard_map/vision_plane/all_to_all | solution.py:316
  90.2 1.0 copy-start.1
  103.6 5.6 %collective-permute-start.4 = (bf16[32,128,128]{2,1,0:T(8,128)(2,1)S(1)}, bf16[32,128,128]{2,1,0:T(8,128)(2,1)S(1)}, u32[]{:S(2)}, u32[]{:S(2)}) collective-permute-start(bf16[32,128,128]{2,1,0:T(8,128)(2,1)S(1)} %bitcast.18), channel_id=1, source_target_pairs={{0,1},{1,0},{2,3},{3,2},{4,5},{5,4},{6,7},{7,6},{8,9},{9,8},{10,11... | collective-permute-start | bytes 3145736 | tf_op jit(solution)/shard_map/cross_attention/ppermute | solution.py:320
  106.9 24.1 %collective-permute-start.3 = (bf16[128,1024]{1,0:T(8,128)(2,1)S(1)}, bf16[128,1024]{1,0:T(8,128)(2,1)S(1)}, u32[]{:S(2)}, u32[]{:S(2)}) collective-permute-start(bf16[128,1024]{1,0:T(8,128)(2,1)S(1)} %self_attention.1), channel_id=1, source_target_pairs={{0,0},{1,384},{2,2},{3,386},{4,4},{5,388},{6,6},{7,390},{8,8},{9,3... | collective-permute-start | bytes 786440 | tf_op jit(solution)/shard_map/ppermute | solution.py:360
  109.2 1.0 copy-start.2
  129.0 8.9 %collective-permute-start.5 = (bf16[128,1024]{1,0:T(8,128)(2,1)S(1)}, bf16[128,1024]{1,0:T(8,128)(2,1)S(1)}, u32[]{:S(2)}, u32[]{:S(2)}) collective-permute-start(bf16[128,1024]{1,0:T(8,128)(2,1)S(1)} %cross_attention.1), channel_id=1, source_target_pairs={{0,0},{1,384},{2,2},{3,386},{4,4},{5,388},{6,6},{7,390},{8,8},{9,3... | collective-permute-start | bytes 786440 | tf_op jit(solution)/shard_map/ppermute | solution.py:360
